TPU v7x, 32 devices: a whole 2x2x4 slice. The times are simulated.
32 devices in a mesh: rep: 4 (over y, x), blk: 2 (over core), tp: 4 (over z).
Axes of the slice: x: 2, y: 2, z: 4, core: 2. Of those that a mesh axis runs over, the one named last changes fastest.
Arguments:
- hidden: bfloat16 [16, 2048], P('rep', 'blk'), may hold values from -64 to 64
- ln_gain: float32 [2, 2048], P(None, 'blk'), may hold values from 0.1 to 1.9
- w_qkv: bfloat16 [2, 2048, 3, 2048], P(None, 'blk', None, 'tp'), may hold values from -0.125 to 0.125
- w_fc1: bfloat16 [2, 2048, 8192], P(None, 'blk', 'tp'), may hold values from -0.125 to 0.125
- w_out: bfloat16 [2, 2048, 2048], P(None, 'tp', 'blk'), may hold values from -0.125 to 0.125
- w_fc2: bfloat16 [2, 8192, 2048], P(None, 'tp', 'blk'), may hold values from -0.0625 to 0.0625
- caches: bfloat16 [2, 2, 64, 32, 2048], P(None, None, ('rep', 'blk'), None, 'tp'), may hold values from -110 to 110
- page_owner: int32 [64], P(('rep', 'blk')), may hold values from 0 to 15, as said below
- page_used: int32 [64], P(('rep', 'blk')), may hold values from 0 to 1, as said below
- page_fill: int32 [64], P(('rep', 'blk')), may hold values from 0 to 32, as said below
- page_tail: int32 [64], P(('rep', 'blk')), may hold values from 0 to 1
- positions: int32 [16], P('rep'), may hold values from 0 to 4095
Outputs:
- hidden_out: bfloat16 [16, 2048], P('rep', 'blk')
- caches_out: bfloat16 [2, 2, 64, 32, 2048], P(None, None, ('rep', 'blk'), None, 'tp')
Inputs may be any that keep to these rules, and one draw needn't show every extreme that they name: `page_owner`: requests are numbered replica by replica, 4 to a replica. Each request has exactly one page with page_tail 1, which is used and lies among the pages of its own replica; other pages of a request may lie on any replica. `page_used`: every page with page_tail 1 is used. `page_fill`: A used page with page_tail 0 is full; a page with page_tail 1 holds fewer than 32 tokens; an unused page holds 0.
All inputs are finite; a program needn't handle non-finite values.
Results may differ from a plain program's by a relative error of at most 0.012.
The roundings to bfloat16 on the way count: a program that leaves them out, or rounds other values in their place, can miss the bound.
Values may be sent and summed in bfloat16 or wider, within the bound.
A program may use at most 64 MiB of HBM per device.

v0:
```python
import jax
import jax.numpy as jnp
from jax import lax
from jax.sharding import PartitionSpec as P

D = 2048
HD = 64
ROT = 32
LAYERS = 2
PAGE = 32


EPSILON = 1e-05
LOWEST = -1e30


def combined_all(value, axis, join):
    pieces = jax.tree.map(lambda part: lax.all_gather(part, axis), value)
    head = jax.tree.map(lambda part: part[0], pieces)
    tail = jax.tree.map(lambda part: part[1:], pieces)
    so_far, _ = lax.scan(lambda so_far, piece: (join(so_far, piece), None), head, tail)
    return so_far


def rotate_heads(tensor, positions):
    half_rot = ROT // 2
    steps_f = jnp.arange(half_rot, dtype=jnp.float32)
    inverse = 10000.0 ** (-2.0 * steps_f / ROT)
    angles = positions.astype(jnp.float32)[:, None] * inverse[None, :]
    cosine = jnp.cos(angles)[:, None, :]
    sine_val = jnp.sin(angles)[:, None, :]
    first_half = tensor[..., :half_rot]
    second_half = tensor[..., half_rot:ROT]
    return jnp.concatenate(
        [
            first_half * cosine - second_half * sine_val,
            second_half * cosine + first_half * sine_val,
            tensor[..., ROT:],
        ],
        axis=-1,
    )


def page_partials(query_rows, key_pages, value_pages, valid):
    scores = jnp.einsum(
        "shd,sphd->shp", query_rows, key_pages, preferred_element_type=jnp.float32
    ) * HD ** (-0.5)
    scores = jnp.where(valid[:, None, :], scores, LOWEST)
    highest = jnp.max(scores, axis=-1)
    weights = jnp.where(valid[:, None, :], jnp.exp(scores - highest[..., None]), 0.0)
    totals = jnp.sum(weights, axis=-1)
    rounded = weights.astype(jnp.bfloat16)
    outputs = jnp.einsum("shp,sphd->shd", rounded, value_pages, preferred_element_type=jnp.float32)
    return (highest, totals, outputs)


def merge_parts(left_part, right_part):
    left_high, left_total, left_out = left_part
    right_high, right_total, right_out = right_part
    joined = jnp.maximum(left_high, right_high)
    left_factor = jnp.exp(left_high - joined)
    right_factor = jnp.exp(right_high - joined)
    return (
        joined,
        left_total * left_factor + right_total * right_factor,
        left_out * left_factor[..., None] + right_out * right_factor[..., None],
    )


def per_device(
    hidden,
    ln_gain,
    w_qkv,
    w_fc1,
    w_out,
    w_fc2,
    caches,
    page_owner,
    page_used,
    page_fill,
    page_tail,
    positions,
):
    req_rows = hidden.shape[0]
    slot_count = page_owner.shape[0]
    width = w_out.shape[1]
    heads = width // HD
    rep_count = lax.axis_size("rep")
    rep_index = lax.axis_index("rep")
    all_reqs = req_rows * rep_count
    offsets = jnp.arange(PAGE, dtype=jnp.int32)
    is_tail = page_tail == 1
    is_used = page_used == 1
    write_at = (offsets[None, :] == page_fill[:, None]) & is_tail[:, None]
    valid = is_used[:, None] & (offsets[None, :] < (page_fill + page_tail)[:, None])
    home_rows = page_owner - rep_index * req_rows
    pick_home = (
        (home_rows[:, None] == jnp.arange(req_rows, dtype=jnp.int32)[None, :]) & is_tail[:, None]
    ).astype(jnp.bfloat16)
    pick_owner = page_owner[:, None] == jnp.arange(all_reqs, dtype=jnp.int32)[None, :]
    pick_query = pick_owner.astype(jnp.bfloat16)
    own_mask = pick_owner & is_used[:, None]
    own_map = own_mask.astype(jnp.float32)
    state = hidden
    cache_list = []
    for layer in range(LAYERS):
        resid = state.astype(jnp.float32)
        average = lax.psum(jnp.sum(resid, axis=-1), "blk") / D
        centered = resid - average[:, None]
        variance = lax.psum(jnp.sum(centered * centered, axis=-1), "blk") / D
        normed = (
            centered * lax.rsqrt(variance + EPSILON)[:, None] * ln_gain[layer][None, :]
        ).astype(jnp.bfloat16)
        qkv_part = jnp.dot(
            normed,
            w_qkv[layer].reshape(normed.shape[1], 3 * width),
            preferred_element_type=jnp.float32,
        )
        inner_part = jnp.dot(normed, w_fc1[layer], preferred_element_type=jnp.float32)
        qkv_full, inner = lax.psum((qkv_part, inner_part), "blk")
        mlp_act = jax.nn.gelu(inner, approximate=True).astype(jnp.bfloat16)
        qkv_full = qkv_full.reshape(req_rows, 3, heads, HD)
        mlp_part = jnp.dot(mlp_act, w_fc2[layer], preferred_element_type=jnp.float32)
        queries = (
            rotate_heads(qkv_full[:, 0], positions).astype(jnp.bfloat16).reshape(req_rows, width)
        )
        new_keys = (
            rotate_heads(qkv_full[:, 1], positions).astype(jnp.bfloat16).reshape(req_rows, width)
        )
        new_values = qkv_full[:, 2].astype(jnp.bfloat16).reshape(req_rows, width)
        gathered = lax.all_gather(queries, "rep", axis=0, tiled=True)
        fresh = jnp.dot(
            pick_home,
            jnp.concatenate([new_keys, new_values], axis=1),
            preferred_element_type=jnp.float32,
        ).astype(jnp.bfloat16)
        key_pages = jnp.where(write_at[:, :, None], fresh[:, None, :width], caches[layer, 0])
        value_pages = jnp.where(write_at[:, :, None], fresh[:, None, width:], caches[layer, 1])
        cache_list.append(jnp.stack([key_pages, value_pages]))
        query_rows = (
            jnp.dot(pick_query, gathered, preferred_element_type=jnp.float32)
            .astype(jnp.bfloat16)
            .reshape(slot_count, heads, HD)
        )
        highest, totals, outputs = page_partials(
            query_rows,
            key_pages.reshape(slot_count, PAGE, heads, HD),
            value_pages.reshape(slot_count, PAGE, heads, HD),
            valid,
        )
        masked_high = jnp.where(is_used[:, None], highest, LOWEST)
        local_high = jnp.max(
            jnp.where(own_mask[:, :, None], masked_high[:, None, :], LOWEST), axis=0
        )
        slot_high = jnp.sum(jnp.where(own_mask[:, :, None], local_high[None, :, :], 0.0), axis=1)
        scale_w = jnp.where(is_used[:, None], jnp.exp(highest - slot_high), 0.0)
        local_total = jnp.einsum(
            "sr,sh->rh", own_map, totals * scale_w, precision=lax.Precision.HIGHEST
        )
        local_out = jnp.einsum(
            "sr,shd->rhd", own_map, outputs * scale_w[..., None], precision=lax.Precision.HIGHEST
        )
        merged_high, merged_total, merged_out = combined_all(
            (local_high, local_total, local_out), ("rep", "blk"), merge_parts
        )
        req_total = lax.dynamic_slice_in_dim(merged_total, rep_index * req_rows, req_rows, 0)
        req_out = lax.dynamic_slice_in_dim(merged_out, rep_index * req_rows, req_rows, 0)
        attended = (req_out / req_total[..., None]).reshape(req_rows, width).astype(jnp.bfloat16)
        attn_part = jnp.dot(attended, w_out[layer], preferred_element_type=jnp.float32)
        branch_total = lax.psum(attn_part + mlp_part, "tp")
        state = (resid + branch_total).astype(jnp.bfloat16)
    return (state, jnp.stack(cache_list))


def solution(mesh):
    in_specs = (
        P("rep", "blk"),
        P(None, "blk"),
        P(None, "blk", None, "tp"),
        P(None, "blk", "tp"),
        P(None, "tp", "blk"),
        P(None, "tp", "blk"),
        P(None, None, ("rep", "blk"), None, "tp"),
        P(("rep", "blk")),
        P(("rep", "blk")),
        P(("rep", "blk")),
        P(("rep", "blk")),
        P("rep"),
    )
    out_specs = (P("rep", "blk"), P(None, None, ("rep", "blk"), None, "tp"))
    return jax.shard_map(
        per_device, mesh=mesh, in_specs=in_specs, out_specs=out_specs, check_vma=False
    )
```

profile of v0, /device:TPU:0, one launch (start us, length us, event | category | flops | bytes accessed | tf_op | source)
XLA Modules:
  0.0 207.9 jit_solution(882762484604758108)
XLA Ops:
  0.6 6.3 %fusion.139 = (bf16[1,1024,3,512]{3,1,2,0:T(8,128)(2,1)}, bf16[1,1024,3,512]{3,1,2,0:T(8,128)(2,1)}) fusion(bf16[2,1024,3,512]{3,1,2,0:T(8,128)(2,1)} %param.18), kind=kLoop, calls=%fused_computation.215 | loop fusion | bytes 12582912 | tf_op jit(solution)/shard_map/slice | solution.py:116
  6.9 3.2 %copy.104 = bf16[1,1024,3,512]{1,3,2,0:T(8,128)(2,1)S(1)} copy(bf16[1,1024,3,512]{3,1,2,0:T(8,128)(2,1)} %get-tuple-element.181) | data formatting | bytes 6291456
  10.1 4.7 %copy.102 = bf16[1,1024,3,512]{1,3,2,0:T(8,128)(2,1)} copy(bf16[1,1024,3,512]{3,1,2,0:T(8,128)(2,1)} %get-tuple-element.180) | data formatting | bytes 6291456
  15.6 2.6 %psum.70 = f32[4]{0:T(128)S(1)} all-reduce(f32[4]{0:T(128)S(1)} %convert_reduce_fusion.1), channel_id=1, replica_groups=mesh['rep'=4,'blk'=2,'tp'=4] {'blk'}, use_global_device_ids=true, to_apply=%region_1.0 | all-reduce | flops 4 | bytes 32 | tf_op jit(solution)/shard_map/psum | solution.py:108
  18.4 2.5 %psum.71 = f32[4]{0:T(128)S(1)} all-reduce(f32[4]{0:T(128)S(1)} %fusion.77), channel_id=1, replica_groups=mesh['rep'=4,'blk'=2,'tp'=4] {'blk'}, use_global_device_ids=true, to_apply=%region_3.0 | all-reduce | flops 4 | bytes 32 | tf_op jit(solution)/shard_map/psum | solution.py:110
  20.8 2.8 %fusion.131 = f32[4,1536]{1,0:T(4,128)S(1)} fusion(bf16[1024,1536]{0,1:T(8,128)(2,1)} %bitcast.148, bf16[4,1024]{1,0:T(4,128)(2,1)S(1)} %copy-done.2, f32[1024]{0:T(1024)S(1)} %bitcast.159, f32[4]{0:T(128)S(1)} %add_rsqrt_fusion.1, f32[4]{0:T(128)S(1)} %broadcast_multiply_fusion.1), kind=kOutput, calls=%fused_computation.213 | convolution fusion | flops 12603392 | bytes 3182624 | tf_op jit(solution)/shard_map/dot_general | solution.py:114
  23.7 2.9 %fusion.14 = f32[4,2048]{1,0:T(4,128)S(1)} fusion(bf16[2,1024,2048]{2,1,0:T(8,128)(2,1)} %param.19, bf16[4,1024]{1,0:T(4,128)(2,1)S(1)} %copy-done.2, f32[1024]{0:T(1024)S(1)} %bitcast.160, f32[4]{0:T(128)S(1)} %add_rsqrt_fusion.1, f32[4]{0:T(128)S(1)} %broadcast_multiply_fusion.1), kind=kOutput, calls=%fused_computation.26 | convolution fusion | flops 16797696 | bytes 4239392 | tf_op jit(solution)/shard_map/dot_general | solution.py:119
  26.6 4.3 %all-reduce.1 = (f32[4,3,8,64]{3,2,1,0:T(8,128)S(1)}, f32[4,2048]{1,0:T(4,128)}) all-reduce(f32[4,3,8,64]{3,2,1,0:T(8,128)S(1)} %reshape.328, f32[4,2048]{1,0:T(4,128)S(1)} %fusion.14), channel_id=1, replica_groups=mesh['rep'=4,'blk'=2,'tp'=4] {'blk'}, use_global_device_ids=true, to_apply=%region_4.0 | all-reduce | flops 14336 | bytes 114688 | tf_op jit(solution)/shard_map/psum | solution.py:120
  31.5 9.3 %all-gather.6 = bf16[4,4,512]{2,1,0:T(4,128)(2,1)S(1)} all-gather(bf16[1,4,512]{2,1,0:T(4,128)(2,1)S(1)} %reshape.356), channel_id=1, replica_groups=mesh['rep'=4,'blk'=2,'tp'=4] {'rep'}, dimensions={0}, use_global_device_ids=true | all-gather | bytes 20480 | tf_op jit(solution)/shard_map/all_gather | solution.py:131
  41.8 2.1 %fusion.140 = (bf16[1,1,8,32,512]{4,3,2,1,0:T(8,128)(2,1)}, bf16[1,1,8,32,512]{4,3,2,1,0:T(8,128)(2,1)}, bf16[1,1,8,32,512]{4,3,2,1,0:T(8,128)(2,1)}, bf16[1,1,8,32,512]{4,3,2,1,0:T(8,128)(2,1)S(1)}) fusion(bf16[2,2,8,32,512]{4,3,2,1,0:T(8,128)(2,1)} %param.22), kind=kLoop, calls=%fused_computation.216 | loop fusion | bytes 2097152 | tf_op jit(solution)/shard_map/slice | solution.py:138
  43.9 2.1 squeeze.95
  47.3 2.1 squeeze.92
  49.4 1.5 broadcast_select_fusion.2
  52.4 9.0 %all-gather.7 = f32[8,16,8]{1,2,0:T(8,128)S(1)} all-gather(f32[1,16,8]{1,2,0:T(8,128)S(1)} %bitcast.156), channel_id=2, replica_groups=mesh['rep'=4,'blk'=2,'tp'=4] {'rep','blk'}, dimensions={0}, use_global_device_ids=true | all-gather | bytes 4608 | tf_op jit(solution)/shard_map/all_gather | solution.py:18
  62.6 8.1 %all-gather.8 = f32[8,16,8]{1,2,0:T(8,128)S(1)} all-gather(f32[1,16,8]{1,2,0:T(8,128)S(1)} %convolution_bitcast_fusion.1), channel_id=3, replica_groups=mesh['rep'=4,'blk'=2,'tp'=4] {'rep','blk'}, dimensions={0}, use_global_device_ids=true | all-gather | bytes 4608 | tf_op jit(solution)/shard_map/all_gather | solution.py:18
  71.3 0.9 fusion.36
  72.2 1.0 fusion.55
  73.3 9.8 %all-gather.2 = f32[128,8,64]{2,0,1:T(8,128)S(1)} all-gather(f32[16,8,64]{2,0,1:T(8,128)S(1)} %fusion.55), channel_id=4, replica_groups=mesh['rep'=4,'blk'=2,'tp'=4] {'rep','blk'}, dimensions={0}, use_global_device_ids=true | all-gather | bytes 294912 | tf_op jit(solution)/shard_map/all_gather | solution.py:18
  85.1 21.7 %while.28 = (s32[]{:T(128)}, f32[16,8]{0,1:T(8,128)}, f32[16,8]{0,1:T(8,128)}, f32[16,8,64]{2,1,0:T(8,128)S(1)}, f32[7,16,8]{1,2,0:T(8,128)}, /*index=5*/f32[7,16,8]{1,2,0:T(8,128)}, f32[7,16,8,64]{3,1,0,2:T(8,128)}, s32[]{:T(128)}) while((s32[]{:T(128)}, f32[16,8]{0,1:T(8,128)}, f32[16,8]{0,1:T(8,128)}, f32[16,8,64]{2,1,0:T(8,128)S(1)}, ...), condition=%wide.region_10.11_spmd, body=%wide.region_9.10_spmd.sunk | while | flops 25346 | bytes 171109 | solution.py:21
  85.1 1.3 fusion.156
  86.5 0.8 constant_dynamic-slice_fusion.6
  88.3 1.3 fusion.156
  89.6 0.8 constant_dynamic-slice_fusion.6
  91.4 1.3 fusion.156
  92.7 0.8 constant_dynamic-slice_fusion.6
  94.5 1.3 fusion.156
  95.8 0.8 constant_dynamic-slice_fusion.6
  97.6 1.3 fusion.156
  98.9 0.8 constant_dynamic-slice_fusion.6
  100.7 1.3 fusion.156
  103.8 1.3 fusion.156
  107.9 1.5 fusion.28
  109.4 2.9 %fusion.20 = f32[4,1024]{1,0:T(4,128)S(1)} fusion(f32[4,1024]{1,0:T(4,128)S(1)} %fusion.28, bf16[2,2048,1024]{2,1,0:T(8,128)(2,1)} %param.21, f32[4,2048]{1,0:T(4,128)} %get-tuple-element.169), kind=kOutput, calls=%fused_computation.34 | convolution fusion | flops 16855040 | bytes 4259840 | tf_op jit(solution)/shard_map/dot_general | solution.py:123
  112.2 19.1 %psum.74 = f32[4,1024]{1,0:T(4,128)S(1)} all-reduce(f32[4,1024]{1,0:T(4,128)S(1)} %fusion.20), channel_id=1, replica_groups=mesh['rep'=4,'blk'=2,'tp'=4] {'tp'}, use_global_device_ids=true, to_apply=%region_12.13 | all-reduce | flops 4096 | bytes 32768 | tf_op jit(solution)/shard_map/psum | solution.py:170
  131.5 2.5 %psum.75 = f32[4]{0:T(128)S(1)} all-reduce(f32[4]{0:T(128)S(1)} %get-tuple-element.178), channel_id=1, replica_groups=mesh['rep'=4,'blk'=2,'tp'=4] {'blk'}, use_global_device_ids=true, to_apply=%region_14.15 | all-reduce | flops 4 | bytes 32 | tf_op jit(solution)/shard_map/psum | solution.py:108
  134.1 2.5 %psum.76 = f32[4]{0:T(128)S(1)} all-reduce(f32[4]{0:T(128)S(1)} %fusion.74), channel_id=1, replica_groups=mesh['rep'=4,'blk'=2,'tp'=4] {'blk'}, use_global_device_ids=true, to_apply=%region_16.17 | all-reduce | flops 4 | bytes 32 | tf_op jit(solution)/shard_map/psum | solution.py:110
  136.6 0.9 fusion.134
  137.7 2.9 %fusion.10 = f32[4,2048]{1,0:T(4,128)S(1)} fusion(bf16[2,1024,2048]{2,1,0:T(8,128)(2,1)} %param.19, bf16[4,1024]{1,0:T(4,128)(2,1)S(1)} %get-tuple-element.179, f32[1024]{0:T(1024)S(1)} %bitcast.158, f32[4]{0:T(128)S(1)} %add_rsqrt_fusion, f32[4]{0:T(128)S(1)} %broadcast_multiply_fusion), kind=kOutput, calls=%fused_computation.22 | convolution fusion | flops 16797696 | bytes 4239392 | tf_op jit(solution)/shard_map/dot_general | solution.py:119
  140.6 3.6 %all-reduce = (f32[4,3,8,64]{3,2,0,1:T(8,128)S(1)}, f32[4,2048]{1,0:T(4,128)S(1)}) all-reduce(f32[4,3,8,64]{3,2,0,1:T(8,128)S(1)} %copy.83, f32[4,2048]{1,0:T(4,128)S(1)} %fusion.10), channel_id=1, replica_groups=mesh['rep'=4,'blk'=2,'tp'=4] {'blk'}, use_global_device_ids=true, to_apply=%region_17.18 | all-reduce | flops 14336 | bytes 114688 | tf_op jit(solution)/shard_map/psum | solution.py:120
  144.6 7.2 %all-gather.9 = bf16[4,4,512]{2,1,0:T(4,128)(2,1)S(1)} all-gather(bf16[1,4,512]{2,1,0:T(4,128)(2,1)S(1)} %reshape.362), channel_id=1, replica_groups=mesh['rep'=4,'blk'=2,'tp'=4] {'rep'}, dimensions={0}, use_global_device_ids=true | all-gather | bytes 20480 | tf_op jit(solution)/shard_map/all_gather | solution.py:131
  155.1 9.1 %all-gather.10 = f32[8,16,8]{1,2,0:T(8,128)S(1)} all-gather(f32[1,16,8]{1,2,0:T(8,128)S(1)} %bitcast.155), channel_id=5, replica_groups=mesh['rep'=4,'blk'=2,'tp'=4] {'rep','blk'}, dimensions={0}, use_global_device_ids=true | all-gather | bytes 4608 | tf_op jit(solution)/shard_map/all_gather | solution.py:18
  164.7 8.3 %all-gather.11 = f32[8,16,8]{1,2,0:T(8,128)S(1)} all-gather(f32[1,16,8]{1,2,0:T(8,128)S(1)} %convolution_bitcast_fusion), channel_id=6, replica_groups=mesh['rep'=4,'blk'=2,'tp'=4] {'rep','blk'}, dimensions={0}, use_global_device_ids=true | all-gather | bytes 4608 | tf_op jit(solution)/shard_map/all_gather | solution.py:18
  173.6 9.8 %all-gather.5 = f32[128,8,64]{2,0,1:T(8,128)S(1)} all-gather(f32[16,8,64]{2,0,1:T(8,128)S(1)} %fusion.54), channel_id=7, replica_groups=mesh['rep'=4,'blk'=2,'tp'=4] {'rep','blk'}, dimensions={0}, use_global_device_ids=true | all-gather | bytes 294912 | tf_op jit(solution)/shard_map/all_gather | solution.py:18
  183.6 2.2 %while.29 = (s32[]{:T(128)}, f32[16,8]{0,1:T(8,128)S(1)}, f32[16,8]{0,1:T(8,128)S(1)}, f32[16,8,64]{2,1,0:T(8,128)S(1)}, f32[7,16,8]{1,2,0:T(8,128)S(1)}, /*inde...) while((s32[]{:T(128)}, f32[16,8]{0,1:T(8,128)S(1)}, f32[16,8]{0,1:T(8,128)S(1)}, ...), condition=%wide.region_23.24_spmd, body=%wide.region_22.23_spmd.sunk | while | flops 25346 | bytes 171109 | solution.py:21
  186.1 1.5 fusion.26
  187.6 2.8 %fusion.23 = f32[4,1024]{1,0:T(4,128)S(1)} fusion(f32[4,1024]{1,0:T(4,128)S(1)} %fusion.26, bf16[2,2048,1024]{2,1,0:T(8,128)(2,1)} %param.21, f32[4,2048]{1,0:T(4,128)S(1)} %get-tuple-element.167), kind=kOutput, calls=%fused_computation.35 | convolution fusion | flops 16855040 | bytes 4259840 | tf_op jit(solution)/shard_map/dot_general | solution.py:123
  190.5 15.5 %psum.79 = f32[4,1024]{1,0:T(4,128)S(1)} all-reduce(f32[4,1024]{1,0:T(4,128)S(1)} %fusion.23), channel_id=1, replica_groups=mesh['rep'=4,'blk'=2,'tp'=4] {'tp'}, use_global_device_ids=true, to_apply=%region_25.26 | all-reduce | flops 4096 | bytes 32768 | tf_op jit(solution)/shard_map/psum | solution.py:170
  206.9 1.1 pad_maximum_fusion
  (228 shorter events, 26.8 us)
Async XLA Ops:
  10.1 4.7 %copy-start.23 = (f32[2,1024]{1,0:T(2,128)S(1)}, f32[2,1024]{1,0:T(2,128)}, u32[]{:S(2)}) copy-start(f32[2,1024]{1,0:T(2,128)} %param.17) | copy-start | bytes 24580
  10.1 5.3 %copy-start.2 = (bf16[4,1024]{1,0:T(4,128)(2,1)S(1)}, bf16[4,1024]{1,0:T(4,128)(2,1)}, u32[]{:S(2)}) copy-start(bf16[4,1024]{1,0:T(4,128)(2,1)} %param.16) | copy-start | bytes 24580
  14.8 16.2 %copy-start.29 = (s32[4]{0:T(128)S(1)}, s32[4]{0:T(128)}, u32[]{:S(2)}) copy-start(s32[4]{0:T(128)} %param.27) | copy-start | bytes 52
  14.8 26.0 %copy-start.25 = (s32[8]{0:T(128)S(1)}, s32[8]{0:T(128)}, u32[]{:S(2)}) copy-start(s32[8]{0:T(128)} %param.23) | copy-start | bytes 100
  23.6 22.3 %copy-start.30 = (s32[8]{0:T(128)S(1)}, s32[8]{0:T(128)}, u32[]{:S(2)}) copy-start(s32[8]{0:T(128)} %param.26) | copy-start | bytes 100
  23.6 22.3 %copy-start.24 = (s32[8]{0:T(128)S(1)}, s32[8]{0:T(128)}, u32[]{:S(2)}) copy-start(s32[8]{0:T(128)} %param.25) | copy-start | bytes 100
  31.0 10.1 %copy-start.9 = (f32[4,3,8,64]{3,2,1,0:T(8,128)}, f32[4,3,8,64]{3,2,1,0:T(8,128)S(1)}, u32[]{:S(2)}) copy-start(f32[4,3,8,64]{3,2,1,0:T(8,128)S(1)} %get-tuple-element.168) | copy-start | bytes 73732
  31.2 18.1 %copy-start.15 = (f32[4,16]{1,0:T(4,128)}, f32[4,16]{1,0:T(4,128)S(1)}, u32[]{:S(2)}) copy-start(f32[4,16]{1,0:T(4,128)S(1)} %get-tuple-element.220) | copy-start | bytes 772
  31.2 18.1 %copy-start.17 = (f32[4,16]{1,0:T(4,128)}, f32[4,16]{1,0:T(4,128)S(1)}, u32[]{:S(2)}) copy-start(f32[4,16]{1,0:T(4,128)S(1)} %get-tuple-element.221) | copy-start | bytes 772
  41.8 9.2 %copy-start.10 = (bf16[8,8,64,1]{2,3,1,0:T(2,128)(2,1)S(1)}, bf16[8,8,64,1]{2,3,1,0:T(2,128)(2,1)}, u32[]{:S(2)}) copy-start(bf16[8,8,64,1]{2,3,1,0:T(2,128)(2,1)} %reshape.392) | copy-start | bytes 24580
  46.0 25.3 %copy-start.27 = (pred[8]{0:T(512)(128)(4,1)}, pred[8]{0:T(512)(128)(4,1)S(1)}, u32[]{:S(2)}) copy-start(pred[8]{0:T(512)(128)(4,1)S(1)} %broadcast_compare_fusion) | copy-start | bytes 28
  46.1 4.8 %copy-start.21 = (pred[8,32]{1,0:T(8,128)(4,1)}, pred[8,32]{1,0:T(8,128)(4,1)S(1)}, u32[]{:S(2)}) copy-start(pred[8,32]{1,0:T(8,128)(4,1)S(1)} %fusion.104) | copy-start | bytes 772
  47.0 3.9 %copy-start.31 = (s32[8]{0:T(128)}, s32[8]{0:T(128)S(1)}, u32[]{:S(2)}) copy-start(s32[8]{0:T(128)S(1)} %broadcast_subtract_fusion) | copy-start | bytes 100
  47.2 5.2 %copy-start.4 = (bf16[8,512]{1,0:T(8,128)(2,1)}, bf16[8,512]{1,0:T(8,128)(2,1)S(1)}, u32[]{:S(2)}) copy-start(bf16[8,512]{1,0:T(8,128)(2,1)S(1)} %get-tuple-element.208) | copy-start | bytes 24580
  47.2 5.2 %copy-start.6 = (bf16[8,512]{1,0:T(8,128)(2,1)}, bf16[8,512]{1,0:T(8,128)(2,1)S(1)}, u32[]{:S(2)}) copy-start(bf16[8,512]{1,0:T(8,128)(2,1)S(1)} %get-tuple-element.209) | copy-start | bytes 24580
  52.0 33.2 %copy-start.19 = (pred[8]{0:T(512)(128)(4,1)}, pred[8]{0:T(512)(128)(4,1)S(1)}, u32[]{:S(2)}) copy-start(pred[8]{0:T(512)(128)(4,1)S(1)} %broadcast_compare_fusion.1) | copy-start | bytes 28
  52.1 20.1 %copy-start.11 = (pred[8,32]{1,0:T(8,128)(4,1)}, pred[8,32]{1,0:T(8,128)(4,1)S(1)}, u32[]{:S(2)}) copy-start(pred[8,32]{1,0:T(8,128)(4,1)S(1)} %fusion.103) | copy-start | bytes 772
  52.3 19.8 %copy-start.13 = (pred[8,16]{1,0:T(8,128)(4,1)}, pred[8,16]{1,0:T(8,128)(4,1)S(1)}, u32[]{:S(2)}) copy-start(pred[8,16]{1,0:T(8,128)(4,1)S(1)} %fusion.102) | copy-start | bytes 388
  106.8 24.5 %copy-start.3 = (bf16[4,1024]{1,0:T(4,128)(2,1)S(1)}, bf16[4,1024]{1,0:T(4,128)(2,1)}, u32[]{:S(2)}) copy-start(bf16[4,1024]{1,0:T(4,128)(2,1)} %param.16) | copy-start | bytes 24580
  106.9 29.8 %copy-start.8 = (f32[1,1024]{1,0:T(1,128)S(1)}, f32[1,1024]{1,0:T(1,128)}, u32[]{:S(2)}) copy-start(f32[1,1024]{1,0:T(1,128)} %get-tuple-element.210) | copy-start | bytes 12292
  112.2 32.1 %copy-start.16 = (f32[4,16]{1,0:T(4,128)S(1)}, f32[4,16]{1,0:T(4,128)}, u32[]{:S(2)}) copy-start(f32[4,16]{1,0:T(4,128)} %copy-done.15) | copy-start | bytes 772
  112.2 32.1 %copy-start.18 = (f32[4,16]{1,0:T(4,128)S(1)}, f32[4,16]{1,0:T(4,128)}, u32[]{:S(2)}) copy-start(f32[4,16]{1,0:T(4,128)} %copy-done.17) | copy-start | bytes 772
  136.6 17.4 %copy-start.22 = (pred[8,32]{1,0:T(8,128)(4,1)S(1)}, pred[8,32]{1,0:T(8,128)(4,1)}, u32[]{:S(2)}) copy-start(pred[8,32]{1,0:T(8,128)(4,1)} %copy-done.21) | copy-start | bytes 772
  137.5 15.2 %copy-start.1 = (bf16[1,1,8,32,512]{4,3,2,1,0:T(8,128)(2,1)S(1)}, bf16[1,1,8,32,512]{4,3,2,1,0:T(8,128)(2,1)}, u32[]{:S(2)}) copy-start(bf16[1,1,8,32,512]{4,3,2,1,0:T(8,128)(2,1)} %get-tuple-element.186) | copy-start | bytes 786436
  137.5 15.8 %copy-start.28 = (pred[8]{0:T(512)(128)(4,1)S(1)}, pred[8]{0:T(512)(128)(4,1)}, u32[]{:S(2)}) copy-start(pred[8]{0:T(512)(128)(4,1)} %copy-done.27) | copy-start | bytes 28
  137.5 15.8 %copy-start.32 = (s32[8]{0:T(128)S(1)}, s32[8]{0:T(128)}, u32[]{:S(2)}) copy-start(s32[8]{0:T(128)} %copy-done.31) | copy-start | bytes 100
  137.7 17.2 %copy-start.12 = (pred[8,32]{1,0:T(8,128)(4,1)S(1)}, pred[8,32]{1,0:T(8,128)(4,1)}, u32[]{:S(2)}) copy-start(pred[8,32]{1,0:T(8,128)(4,1)} %copy-done.11) | copy-start | bytes 772
  137.7 17.3 %copy-start.20 = (pred[8]{0:T(512)(128)(4,1)S(1)}, pred[8]{0:T(512)(128)(4,1)}, u32[]{:S(2)}) copy-start(pred[8]{0:T(512)(128)(4,1)} %copy-done.19) | copy-start | bytes 28
  137.7 17.4 %copy-start.14 = (pred[8,16]{1,0:T(8,128)(4,1)S(1)}, pred[8,16]{1,0:T(8,128)(4,1)}, u32[]{:S(2)}) copy-start(pred[8,16]{1,0:T(8,128)(4,1)} %copy-done.13) | copy-start | bytes 388
  137.7 26.8 %copy-start.26 = (s32[8]{0:T(128)S(1)}, s32[8]{0:T(128)}, u32[]{:S(2)}) copy-start(s32[8]{0:T(128)} %param.23) | copy-start | bytes 100
  183.5 23.1 %copy-start = (bf16[2,2,8,32,512]{4,3,2,1,0:T(8,128)(2,1)S(1)}, bf16[2,2,8,32,512]{4,3,2,1,0:T(8,128)(2,1)}, u32[]{:S(2)}) copy-start(bf16[2,2,8,32,512]{4,3,2,1,0:T(8,128)(2,1)} %param.22) | copy-start | bytes 3145732
  183.5 23.1 %copy-start.5 = (bf16[8,512]{1,0:T(8,128)(2,1)S(1)}, bf16[8,512]{1,0:T(8,128)(2,1)}, u32[]{:S(2)}) copy-start(bf16[8,512]{1,0:T(8,128)(2,1)} %copy-done.4) | copy-start | bytes 24580
  183.5 23.1 %copy-start.7 = (bf16[8,512]{1,0:T(8,128)(2,1)S(1)}, bf16[8,512]{1,0:T(8,128)(2,1)}, u32[]{:S(2)}) copy-start(bf16[8,512]{1,0:T(8,128)(2,1)} %copy-done.6) | copy-start | bytes 24580
where the time goes:
time: 210 us; the launch traced here: 208 us
  blocking collectives  123 us (59%)
  local copies, waits for them, and re-layouts  42 us (20%)
  matrix products  23.1 us (11%)
  other arithmetic  18.1 us (9%)
    all_gather x6, blocking collectives, combined_all(): pieces = jax.tree.map(lambda part: lax.all_gather(part, axis), value)  54.2 us
    psum x2, blocking collectives, per_device(): branch_total = lax.psum(attn_part + mlp_part, 'tp')  34.7 us
    all_gather x2, blocking collectives, per_device(): gathered = lax.all_gather(queries, 'rep', axis=0, tiled=True)  16.5 us
    add x14, other arithmetic, merge_parts(): left_total * left_factor + right_total * right_factor  9.28 us
    unnamed x72, local copies, waits for them, and re-layouts  8.22 us
    psum x2, blocking collectives, per_device(): qkv_full, inner = lax.psum((qkv_part, inner_part), 'blk')  7.97 us
    slice x1, local copies, waits for them, and re-layouts, per_device(): w_qkv[layer].reshape(normed.shape[1], 3 * width)  6.3 us
    dynamic_slice x14, local copies, waits for them, and re-layouts, combined_all(): lax.scan(lambda so_far, piece: (join(so_far, piece), None), head, tail)  6.01 us

commit v1 on v0

v1 whole, which is shorter than its diff:
```python
import functools

import jax
import jax.numpy as jnp
import numpy as np
from jax import lax
from jax.experimental import pallas as pl
from jax.experimental.pallas import tpu as pltpu
from jax.sharding import PartitionSpec as P

HD = 64
ROT = 32
LAYERS = 2
PAGE = 32
EPSILON = 1e-05
LOWEST = -1e30
MESH = pl.DeviceIdType.MESH
UNROLL = 8


def each(start, stop, body):
    if stop - start <= UNROLL:
        for k in range(start, stop):
            body(k)
    else:
        lax.fori_loop(start, stop, lambda k, c: (body(k), c)[1], 0)


def fold_sum(start, stop, body, carry):
    if stop - start <= UNROLL:
        for k in range(start, stop):
            carry = body(k, carry)
        return carry
    return lax.fori_loop(start, stop, body, carry)


def lane_iota(shape):
    return lax.broadcasted_iota(jnp.int32, shape, len(shape) - 1)


def row_iota(shape):
    return lax.broadcasted_iota(jnp.int32, shape, len(shape) - 2)


def kernel(
    n_rep, n_blk, n_tp,
    owner_ref, used_ref, fill_ref, tail_ref, pos_ref,
    hidden_ref, gain_ref, freq_ref,
    wqkv_hbm, wfc1_hbm, wout_hbm, wfc2_hbm, cache_hbm,
    state_ref, fresh_ref,
    wqkv, wfc1, wout, wfc2, cache,
    buf_a, buf_i, buf_q, msg, buf_b, buf_c, mlp_acc, act_ref,
    w_sem, a_send, a_recv, i_send, i_recv, q_send, q_recv, b_send, b_recv, c_send, c_recv,
):
    f32, bf16 = jnp.float32, jnp.bfloat16
    rows, model = hidden_ref.shape
    full_model = model * n_blk
    slots = owner_ref.shape[0]
    width = wout.shape[1]
    heads = width // HD
    n_ff = wfc1.shape[1]
    reqs = rows * n_rep
    n_all = n_rep * n_blk
    half = width // 2
    my_rep, my_blk, my_tp = lax.axis_index("rep"), lax.axis_index("blk"), lax.axis_index("tp")
    my_flat = my_rep * n_blk + my_blk
    ff_half = n_ff // 2

    local = []

    def bring(src, dst):
        copy = pltpu.make_async_copy(src, dst, w_sem.at[len(local)])
        copy.start()
        local.append(copy)
        return copy

    got = []
    for l in range(LAYERS):
        g = {}
        g["qkv"] = [bring(wqkv_hbm.at[l, j], wqkv.at[l, j]) for j in range(3)]
        g["fc1"] = [
            bring(wfc1_hbm.at[l, :, pl.ds(c * width, width)], wfc1.at[l, c]) for c in range(n_ff)
        ]
        g["cache"] = [bring(cache_hbm.at[l, i], cache.at[l, i]) for i in range(2)]
        g["fc2"] = [
            bring(wfc2_hbm.at[l, pl.ds(i * ff_half * width, ff_half * width), :], wfc2.at[l, i])
            for i in range(2)
        ]
        g["out"] = [bring(wout_hbm.at[l], wout.at[l])]
        got.append(g)

    def flat_peer(k):
        to = lax.rem(my_flat + k, n_all)
        return {"rep": to // n_blk, "blk": lax.rem(to, n_blk)}

    def blk_peer(k):
        return {"blk": lax.rem(my_blk + k, n_blk)}

    def rep_peer(k):
        return {"rep": lax.rem(my_rep + k, n_rep)}

    def tp_peer(k):
        return {"tp": lax.rem(my_tp + k, n_tp)}

    barrier = pltpu.get_barrier_semaphore()
    each(1, n_all, lambda k: pl.semaphore_signal(
        barrier, inc=1, device_id=flat_peer(k), device_id_type=MESH))
    each(1, n_tp, lambda k: pl.semaphore_signal(
        barrier, inc=1, device_id=tp_peer(k), device_id_type=MESH))

    def remote(src, dst, ssem, rsem, peer):
        return pltpu.make_async_remote_copy(
            src_ref=src, dst_ref=dst, send_sem=ssem, recv_sem=rsem,
            device_id=peer, device_id_type=MESH)

    def copy_a(l):
        return lambda k: remote(
            buf_a.at[l, 0], buf_a.at[l, k], a_send.at[l, k], a_recv.at[l, k], blk_peer(k))

    def copy_i(l):
        return lambda k: remote(
            buf_i.at[l, 0], buf_i.at[l, k], i_send.at[l, k], i_recv.at[l, k], blk_peer(k))

    def copy_q(l):
        return lambda k: remote(
            buf_q.at[l, 0], buf_q.at[l, k], q_send.at[l, k], q_recv.at[l, k], rep_peer(k))

    def copy_b(l):
        return lambda k: remote(
            msg.at[l, lax.rem(my_flat + k, n_all) // n_blk], buf_b.at[l, k],
            b_send.at[l, k], b_recv.at[l, k], flat_peer(k))

    def copy_c(l):
        return lambda k: remote(
            buf_c.at[l, 0], buf_c.at[l, k], c_send.at[l, k], c_recv.at[l, k], tp_peer(k))

    feature = lax.rem(lane_iota((2 * rows, width)), HD)
    small = (2 * rows, 128)
    posv = jnp.zeros(small, f32)
    for r in range(rows):
        posv = jnp.where(
            lax.rem(row_iota(small), rows) == r, pos_ref[r].astype(f32), posv)
    angles = posv * freq_ref[...]
    cosine = jnp.concatenate([jnp.cos(angles)] * (width // 128), axis=1)
    sine = jnp.concatenate([jnp.sin(angles)] * (width // 128), axis=1)
    sine = jnp.where(feature < ROT // 2, -sine, sine)

    columns = slots * PAGE
    lanes = lane_iota((1, columns))
    col_owner = jnp.full((1, columns), -1, jnp.int32)
    home = jnp.full((slots, width), -1, jnp.int32)
    write_pos = []
    for s in range(slots):
        limit = jnp.where(used_ref[s] == 1, fill_ref[s] + tail_ref[s], 0)
        here = (lanes >= s * PAGE) & (lanes < s * PAGE + limit)
        col_owner = jnp.where(here, owner_ref[s], col_owner)
        home_row = jnp.where(tail_ref[s] == 1, owner_ref[s] - my_rep * rows, -1)
        home = jnp.where(row_iota((slots, width)) == s, home_row, home)
        write_pos.append(jnp.where(tail_ref[s] == 1, fill_ref[s], -1))

    head_of_lane = lane_iota((1, width)) // HD

    def expand(stat):
        out = jnp.broadcast_to(stat[:, 0:1], (stat.shape[0], width))
        for h in range(1, heads):
            out = jnp.where(head_of_lane == h, stat[:, h:h + 1], out)
        return out

    def fold(x):
        return jnp.concatenate([x[:, :x.shape[1] // 2], x[:, x.shape[1] // 2:]], axis=0)

    def unfold(x):
        return jnp.concatenate([x[:rows], x[rows:]], axis=1)

    state = hidden_ref[...].astype(f32)
    for l in range(LAYERS):
        g = got[l]
        own_mean = jnp.sum(state, axis=1, keepdims=True) / model
        centered = state - own_mean
        own_square = jnp.sum(centered * centered, axis=1, keepdims=True)
        gain = gain_ref[l:l + 1, :]
        gain_hi = gain.astype(bf16).astype(f32)
        gain_lo = gain - gain_hi
        lhs = jnp.concatenate(
            [centered * gain, gain_hi, gain_lo, jnp.zeros((2 * rows - rows - 2, model), f32)],
            axis=0).astype(bf16)
        stat_lane = lane_iota((rows, width))
        stats = jnp.where(stat_lane < 128, own_mean, own_square)
        buf_a[l, 0, 3] = jnp.concatenate([stats, jnp.zeros((rows, width), f32)], axis=0)
        for j in range(3):
            g["qkv"][j].wait()
            buf_a[l, 0, j] = jnp.dot(lhs, wqkv[l, j], preferred_element_type=f32)
        if l == 0:
            pl.semaphore_wait(barrier, n_all - 1 + n_tp - 1)
        each(1, n_blk, lambda k: copy_a(l)(k).start())
        for c in range(n_ff):
            g["fc1"][c].wait()
            buf_i[l, 0, c] = jnp.dot(lhs, wfc1[l, c], preferred_element_type=f32)
        each(1, n_blk, lambda k: copy_i(l)(k).start())

        each(1, n_blk, lambda k: copy_a(l)(k).wait_recv())
        mean = fold_sum(0, n_blk, lambda k, t: t + buf_a[l, k, 3, 0:rows, 0:1],
                        jnp.zeros((rows, 1), f32)) / n_blk

        def add_square(k, total):
            off = buf_a[l, k, 3, 0:rows, 0:1] - mean
            return total + (buf_a[l, k, 3, 0:rows, 128:129] + model * (off * off))

        square = fold_sum(0, n_blk, add_square, jnp.zeros((rows, 1), f32))
        scale = lax.rsqrt(square / full_model + EPSILON)

        def finish(buf, j):
            def add(k, total):
                off = buf_a[l, k, 3, 0:rows, 0:1] - mean
                block = buf[l, k, j]
                gained = block[rows:rows + 1] + block[rows + 1:rows + 2]
                return total + (block[0:rows] + off * gained)

            return fold_sum(0, n_blk, add, jnp.zeros((rows, width), f32)) * scale

        qk = jnp.concatenate([finish(buf_a, 0), finish(buf_a, 1)], axis=0)
        turned = jnp.where(
            feature < ROT // 2,
            pltpu.roll(qk, width - ROT // 2, 1),
            pltpu.roll(qk, ROT // 2, 1))
        qk = (qk * cosine + turned * sine).astype(bf16).astype(f32)
        buf_q[l, 0] = fold(qk[:rows])
        each(1, n_rep, lambda k: copy_q(l)(k).start())
        new_k = qk[rows:]
        new_v = finish(buf_a, 2).astype(bf16).astype(f32)

        for i, new in ((0, new_k), (1, new_v)):
            fresh = jnp.zeros((slots, width), f32)
            for r in range(rows):
                fresh = jnp.where(home == r, new[r:r + 1], fresh)
            fresh_ref[l, i] = fresh
            g["cache"][i].wait()
            for s in range(slots):
                page = cache[l, i, s].astype(f32)
                page = jnp.where(
                    row_iota((PAGE, width)) == write_pos[s], fresh[s:s + 1], page)
                cache[l, i, s] = page.astype(bf16)

        each(1, n_blk, lambda k: copy_i(l)(k).wait_recv())
        for c in range(n_ff):
            act = jax.nn.gelu(finish(buf_i, c), approximate=True)
            act_ref[c] = jnp.concatenate([act, jnp.zeros((rows, width), f32)], axis=0).astype(bf16)
        g["fc2"][0].wait()
        mlp_acc[...] = jnp.dot(
            jnp.concatenate([act_ref[c] for c in range(ff_half)], axis=1),
            wfc2[l, 0], preferred_element_type=f32)

        each(1, n_rep, lambda k: copy_q(l)(k).wait_recv())
        queries = jnp.concatenate(
            [unfold(buf_q[l, lax.rem(my_rep - t + n_rep, n_rep)]) for t in range(n_rep)], axis=0)
        by_head = jnp.concatenate(
            [jnp.where(head_of_lane == h, queries, 0.0) for h in range(heads)], axis=0
        ).astype(bf16)
        keys = cache[l, 0].reshape(columns, width)
        values = cache[l, 1].reshape(columns, width)
        scores = lax.dot_general(
            by_head, keys, (((1,), (1,)), ((), ())), preferred_element_type=f32) * HD ** (-0.5)
        mask = lax.rem(row_iota((heads * reqs, columns)), reqs) == col_owner
        scores = jnp.where(mask, scores, LOWEST)
        highest = jnp.max(scores, axis=1, keepdims=True)
        weights = jnp.where(mask, jnp.exp(scores - highest), 0.0)
        totals = jnp.sum(weights, axis=1, keepdims=True)
        spread = jnp.dot(weights.astype(bf16), values, preferred_element_type=f32)
        out = spread[0:reqs]
        stat_shape = (reqs, 128)
        high_stat = jnp.zeros(stat_shape, f32)
        total_stat = jnp.ones(stat_shape, f32)
        for h in range(heads):
            part = slice(h * reqs, (h + 1) * reqs)
            if h > 0:
                out = jnp.where(head_of_lane == h, spread[part], out)
            high_stat = jnp.where(lane_iota(stat_shape) == h, highest[part], high_stat)
            total_stat = jnp.where(lane_iota(stat_shape) == h, totals[part], total_stat)
        for r in range(n_rep):
            part = slice(r * rows, (r + 1) * rows)
            msg[l, r, :, 0:half] = fold(out[part])
            msg[l, r, :, half:half + 128] = jnp.concatenate(
                [high_stat[part], total_stat[part]], axis=0)
        each(1, n_all, lambda k: copy_b(l)(k).start())
        buf_b[l, 0] = msg[l, my_rep]

        g["fc2"][1].wait()
        mlp_acc[...] += jnp.dot(
            jnp.concatenate([act_ref[c] for c in range(ff_half, n_ff)], axis=1),
            wfc2[l, 1], preferred_element_type=f32)

        each(1, n_all, lambda k: copy_b(l)(k).wait_recv())
        top = fold_sum(
            0, n_all,
            lambda k, t: jnp.maximum(t, buf_b[l, k, 0:rows, half:half + 128]),
            jnp.full((rows, 128), LOWEST, f32))

        def merge(k, carry):
            denom, numer = carry
            factor = jnp.exp(buf_b[l, k, 0:rows, half:half + 128] - top)
            denom = denom + factor * buf_b[l, k, rows:2 * rows, half:half + 128]
            numer = numer + expand(factor) * unfold(buf_b[l, k, :, 0:half])
            return denom, numer

        denom, numer = fold_sum(
            0, n_all, merge, (jnp.zeros((rows, 128), f32), jnp.zeros((rows, width), f32)))
        attended = numer / expand(denom)
        attended = jnp.concatenate(
            [attended, jnp.zeros((rows, width), f32)], axis=0).astype(bf16)
        g["out"][0].wait()
        branch = (
            jnp.dot(attended, wout[l], preferred_element_type=f32) + mlp_acc[...])[0:rows]
        folded = model >= 256
        if folded:
            buf_c[l, 0] = fold(branch)
        else:
            buf_c[l, 0] = jnp.zeros(buf_c.shape[2:], f32)
            buf_c[l, 0, 0:rows, 0:model] = branch
        each(1, n_tp, lambda k: copy_c(l)(k).start())
        each(1, n_tp, lambda k: copy_c(l)(k).wait_recv())
        total = buf_c[l, lax.rem(my_tp + n_tp, n_tp)]
        for t in range(1, n_tp):
            total = total + buf_c[l, lax.rem(my_tp - t + n_tp, n_tp)]
        total = unfold(total) if folded else total[0:rows, 0:model]
        state = (state + total).astype(bf16).astype(f32)

    state_ref[...] = state
    for l in range(LAYERS):
        each(1, n_blk, lambda k: copy_a(l)(k).wait_send())
        each(1, n_blk, lambda k: copy_i(l)(k).wait_send())
        each(1, n_rep, lambda k: copy_q(l)(k).wait_send())
        each(1, n_all, lambda k: copy_b(l)(k).wait_send())
        each(1, n_tp, lambda k: copy_c(l)(k).wait_send())


def frequencies(rows):
    feature = np.arange(128) % HD
    power = 10000.0 ** (-2.0 * (feature % (ROT // 2)) / ROT)
    return np.tile(np.where(feature < ROT, power, 0.0).astype(np.float32)[None, :], (rows, 1))


def per_device(
    hidden, ln_gain, w_qkv, w_fc1, w_out, w_fc2, caches,
    page_owner, page_used, page_fill, page_tail, positions,
):
    n_rep, n_blk, n_tp = (lax.axis_size(a) for a in ("rep", "blk", "tp"))
    f32, bf16 = jnp.float32, jnp.bfloat16
    rows, model = hidden.shape
    slots = page_owner.shape[0]
    width = w_out.shape[1]
    n_ff = w_fc1.shape[2] // width
    n_all = n_rep * n_blk
    wq = jnp.transpose(w_qkv, (0, 2, 1, 3))
    c_width = model // 2 if model >= 256 else 128
    smem = pl.BlockSpec(memory_space=pltpu.SMEM)
    vmem = pl.BlockSpec(memory_space=pltpu.VMEM)
    anywhere = pl.BlockSpec(memory_space=pl.ANY)
    dma = pltpu.SemaphoreType.DMA
    n_copies = LAYERS * (3 + n_ff + 2 + 2 + 1)
    state, fresh = pl.pallas_call(
        functools.partial(kernel, n_rep, n_blk, n_tp),
        out_shape=(
            jax.ShapeDtypeStruct((rows, model), f32),
            jax.ShapeDtypeStruct((LAYERS, 2, slots, width), f32),
        ),
        in_specs=[smem] * 5 + [vmem] * 3 + [anywhere] * 5,
        out_specs=(vmem, vmem),
        scratch_shapes=[
            pltpu.VMEM((LAYERS, 3, model, width), bf16),
            pltpu.VMEM((LAYERS, n_ff, model, width), bf16),
            pltpu.VMEM((LAYERS, width, model), bf16),
            pltpu.VMEM((LAYERS, 2, n_ff // 2 * width, model), bf16),
            pltpu.VMEM((LAYERS, 2, slots, PAGE, width), bf16),
            pltpu.VMEM((LAYERS, n_blk, 4, 2 * rows, width), f32),
            pltpu.VMEM((LAYERS, n_blk, n_ff, 2 * rows, width), f32),
            pltpu.VMEM((LAYERS, n_rep, 2 * rows, width // 2), f32),
            pltpu.VMEM((LAYERS, n_rep, 2 * rows, width // 2 + 128), f32),
            pltpu.VMEM((LAYERS, n_all, 2 * rows, width // 2 + 128), f32),
            pltpu.VMEM((LAYERS, n_tp, 2 * rows, c_width), f32),
            pltpu.VMEM((2 * rows, model), f32),
            pltpu.VMEM((n_ff, 2 * rows, width), bf16),
            dma((n_copies,)),
            dma((LAYERS, n_blk)), dma((LAYERS, n_blk)),
            dma((LAYERS, n_blk)), dma((LAYERS, n_blk)),
            dma((LAYERS, n_rep)), dma((LAYERS, n_rep)),
            dma((LAYERS, n_all)), dma((LAYERS, n_all)),
            dma((LAYERS, n_tp)), dma((LAYERS, n_tp)),
        ],
        compiler_params=pltpu.CompilerParams(
            collective_id=0, has_side_effects=True, vmem_limit_bytes=56 * 2**20),
        name="decode_layers",
    )(
        page_owner, page_used, page_fill, page_tail, positions,
        hidden, ln_gain, jnp.asarray(frequencies(2 * rows)),
        wq, w_fc1, w_out, w_fc2, caches,
    )
    offsets = jnp.arange(PAGE, dtype=jnp.int32)
    write_at = (offsets[None, :] == page_fill[:, None]) & (page_tail == 1)[:, None]
    caches_out = jnp.where(
        write_at[None, None, :, :, None], fresh[:, :, :, None, :].astype(bf16), caches)
    return (state.astype(bf16), caches_out)


def solution(mesh):
    in_specs = (
        P("rep", "blk"),
        P(None, "blk"),
        P(None, "blk", None, "tp"),
        P(None, "blk", "tp"),
        P(None, "tp", "blk"),
        P(None, "tp", "blk"),
        P(None, None, ("rep", "blk"), None, "tp"),
        P(("rep", "blk")),
        P(("rep", "blk")),
        P(("rep", "blk")),
        P(("rep", "blk")),
        P("rep"),
    )
    out_specs = (P("rep", "blk"), P(None, None, ("rep", "blk"), None, "tp"))
    return jax.shard_map(
        per_device, mesh=mesh, in_specs=in_specs, out_specs=out_specs, check_vma=False
    )
```

time: 210 us -> 39.3 us (0.19)
  blocking collectives: 123 us -> 0 us
  local copies, waits for them, and re-layouts: 42 us -> 0.01 us
  Pallas kernels: 0 us -> 33.7 us
  matrix products: 23.1 us -> 0 us
  other arithmetic: 18.1 us -> 4.67 us
    all_gather x8 -> x0, blocking collectives: 70.7 us -> none  [the longest x6 54.2 us: combined_all(): pieces = jax.tree.map(lambda part: lax.all_gather(part, axis), value)]
    psum x8 -> x0, blocking collectives: 52.6 us -> none  [the longest x2 34.7 us: per_device(): branch_total = lax.psum(attn_part + mlp_part, 'tp')]
    pallas_call x0 -> x1, Pallas kernels: none -> 33.7 us  [per_device(): pl.pallas_call(functools.partial(kernel, n_rep, n_blk, n_tp), out_shape=(...]
    dot_general x20 -> x0, matrix products: 23.1 us -> none  [the longest x2 5.76 us: per_device(): jnp.dot(normed, w_fc1[layer], preferred_element_type=jnp.float32)]
    slice x23 -> x0, local copies, waits for them, and re-layouts: 13.3 us -> none  [the longest x1 6.3 us: per_device(): w_qkv[layer].reshape(normed.shape[1], 3 * width)]
    add x29 -> x0, other arithmetic: 10.8 us -> none  [the longest x14 9.28 us: merge_parts(): left_total * left_factor + right_total * right_factor]
    unnamed x72 -> x2, local copies, waits for them, and re-layouts: 8.22 us -> 0.01 us
    dynamic_slice x18 -> x0, local copies, waits for them, and re-layouts: 7.01 us -> none  [the longest x14 6.01 us: combined_all(): lax.scan(lambda so_far, piece: (join(so_far, piece), None), head, tail)]
where the time goes in v1:
time: 39.3 us; the launch traced here: 39 us
  Pallas kernels  33.7 us (86%)
  other arithmetic  4.67 us (12%)
  between operations  0.64 us (2%)
    pallas_call x1, Pallas kernels, per_device(): pl.pallas_call(functools.partial(kernel, n_rep, n_blk, n_tp), out_shape=(...  33.7 us
    convert_element_type x1, other arithmetic, per_device(): return (state.astype(bf16), caches_out)  1.32 us
    select_n x1, other arithmetic, per_device(): jnp.where(write_at[None, None, :, :, None], fresh[:, :, :, None, :].astyp...  1.12 us
    convert_element_type x1, other arithmetic, per_device(): fresh[:, :, :, None, :].astype(bf16)  0.84 us

profile of v1, /device:TPU:0, one launch (start us, length us, event | category | flops | bytes accessed | tf_op | source)
XLA Modules:
  0.0 39.0 jit_solution(3454949115457499693)
XLA Ops:
  0.6 0.7 %broadcast_compare_fusion = pred[8]{0:T(512)(128)(4,1)S(1)} fusion(s32[8]{0:T(128)} %tail_ref.1), kind=kLoop, calls=%fused_computation.3 | loop fusion | flops 8 | bytes 40 | tf_op jit(solution)/shard_map/eq | solution.py:398
  1.3 0.7 %fusion = pred[8,32]{1,0:T(8,128)(4,1)S(1)} fusion(s32[8]{0:T(128)} %fill_ref.1, pred[8]{0:T(512)(128)(4,1)S(1)} %broadcast_compare_fusion), kind=kLoop, calls=%fused_computation.2 | loop fusion | flops 512 | bytes 296 | tf_op jit(solution)/shard_map/and | solution.py:398
  2.0 0.0 copy-start
  2.0 33.7 %decode_layers.1 = (f32[4,1024]{1,0:T(4,128)}, f32[2,2,8,512]{3,2,1,0:T(8,128)}) custom-call(s32[8]{0:T(128)} %owner_ref.1, s32[8]{0:T(128)} %used_ref.1, s32[8]{0:T(128)} %fill_ref.1, s32[8]{0:T(128)} %tail_ref.1, s32[4]{0:T(128)} %pos_ref.1, bf16[4,1024]{1,0:T(4,128)(2,1)} %hidden_ref.1, f32[2,1024]{1,0:T(2,128)} %gain_ref.1, ...), custom_call_target="tpu_custom_call" | custom-call | tf_op jit(solution)/shard_map/decode_layers/pallas_call | solution.py:360
  35.7 1.3 %convert_element_type.7 = bf16[4,1024]{1,0:T(4,128)(2,1)} convert(f32[4,1024]{1,0:T(4,128)} %get-tuple-element.4) | non-fusion elementwise | flops 4096 | bytes 24576 | tf_op jit(solution)/shard_map/convert_element_type | solution.py:401
  37.0 0.8 %convert_element_type.8 = bf16[2,2,8,512]{3,2,1,0:T(8,128)(2,1)S(1)} convert(f32[2,2,8,512]{3,2,1,0:T(8,128)} %get-tuple-element.5) | non-fusion elementwise | flops 16384 | bytes 98304 | tf_op jit(solution)/shard_map/convert_element_type | solution.py:400
  37.9 0.0 copy-done
  37.9 1.1 %broadcast_select_fusion = bf16[2,2,8,32,512]{4,3,2,1,0:T(8,128)(2,1)} fusion(bf16[2,2,8,32,512]{4,3,2,1,0:T(8,128)(2,1)S(1)} %copy-done, pred[8,32]{1,0:T(8,128)(4,1)S(1)} %fusion, bf16[2,2,8,512]{3,2,1,0:T(8,128)(2,1)S(1)} %convert_element_type.8), kind=kLoop, calls=%fused_computation | loop fusion | flops 524288 | bytes 2130176 | tf_op jit(solution)/shard_map/jit(_where)/select_n | solution.py:399
Async XLA Ops:
  2.0 35.8 %copy-start = (bf16[2,2,8,32,512]{4,3,2,1,0:T(8,128)(2,1)S(1)}, bf16[2,2,8,32,512]{4,3,2,1,0:T(8,128)(2,1)}, u32[]{:S(2)}) copy-start(bf16[2,2,8,32,512]{4,3,2,1,0:T(8,128)(2,1)} %cache_hbm.1) | copy-start | bytes 3145732

commit v2 on v1

--- a/solution.py
+++ b/solution.py
@@ -47,10 +47,10 @@
     owner_ref, used_ref, fill_ref, tail_ref, pos_ref,
     hidden_ref, gain_ref, freq_ref,
     wqkv_hbm, wfc1_hbm, wout_hbm, wfc2_hbm, cache_hbm,
-    state_ref, fresh_ref,
+    state_ref, pages_ref,
     wqkv, wfc1, wout, wfc2, cache,
-    buf_a, buf_i, buf_q, msg, buf_b, buf_c, mlp_acc, act_ref,
-    w_sem, a_send, a_recv, i_send, i_recv, q_send, q_recv, b_send, b_recv, c_send, c_recv,
+    buf_a, buf_i, buf_q, msg, buf_b, buf_c, mlp_acc, act_ref, mask_ref,
+    w_sem, o_sem, a_send, a_recv, i_send, i_recv, q_send, q_recv, b_send, b_recv, c_send, c_recv,
 ):
     f32, bf16 = jnp.float32, jnp.bfloat16
     rows, model = hidden_ref.shape
@@ -58,7 +58,7 @@
     slots = owner_ref.shape[0]
     width = wout.shape[1]
     heads = width // HD
-    n_ff = wfc1.shape[1]
+    n_ff = wfc1.shape[2] // width
     reqs = rows * n_rep
     n_all = n_rep * n_blk
     half = width // 2
@@ -66,6 +66,25 @@
     my_flat = my_rep * n_blk + my_blk
     ff_half = n_ff // 2
 
+    def flat_peer(k):
+        to = lax.rem(my_flat + k, n_all)
+        return {"rep": to // n_blk, "blk": lax.rem(to, n_blk)}
+
+    def blk_peer(k):
+        return {"blk": lax.rem(my_blk + k, n_blk)}
+
+    def rep_peer(k):
+        return {"rep": lax.rem(my_rep + k, n_rep)}
+
+    def tp_peer(k):
+        return {"tp": lax.rem(my_tp + k, n_tp)}
+
+    barrier = pltpu.get_barrier_semaphore()
+    each(1, n_all, lambda k: pl.semaphore_signal(
+        barrier, inc=1, device_id=flat_peer(k), device_id_type=MESH))
+    each(1, n_tp, lambda k: pl.semaphore_signal(
+        barrier, inc=1, device_id=tp_peer(k), device_id_type=MESH))
+
     local = []
 
     def bring(src, dst):
@@ -74,39 +93,25 @@
         local.append(copy)
         return copy
 
-    got = []
-    for l in range(LAYERS):
+    def bring_layer(l, pieces):
         g = {}
         g["qkv"] = [bring(wqkv_hbm.at[l, j], wqkv.at[l, j]) for j in range(3)]
+        step = n_ff // pieces
         g["fc1"] = [
-            bring(wfc1_hbm.at[l, :, pl.ds(c * width, width)], wfc1.at[l, c]) for c in range(n_ff)
+            bring(wfc1_hbm.at[l, :, pl.ds(c * width, step * width)],
+                  wfc1.at[l, :, pl.ds(c * width, step * width)])
+            if c % step == 0 else None for c in range(n_ff)
         ]
-        g["cache"] = [bring(cache_hbm.at[l, i], cache.at[l, i]) for i in range(2)]
+        g["cache"] = [
+            bring(cache_hbm.at[l, i], cache.at[l, i, pl.ds(0, slots)]) for i in range(2)]
         g["fc2"] = [
             bring(wfc2_hbm.at[l, pl.ds(i * ff_half * width, ff_half * width), :], wfc2.at[l, i])
             for i in range(2)
         ]
         g["out"] = [bring(wout_hbm.at[l], wout.at[l])]
-        got.append(g)
-
-    def flat_peer(k):
-        to = lax.rem(my_flat + k, n_all)
-        return {"rep": to // n_blk, "blk": lax.rem(to, n_blk)}
-
-    def blk_peer(k):
-        return {"blk": lax.rem(my_blk + k, n_blk)}
-
-    def rep_peer(k):
-        return {"rep": lax.rem(my_rep + k, n_rep)}
-
-    def tp_peer(k):
-        return {"tp": lax.rem(my_tp + k, n_tp)}
-
-    barrier = pltpu.get_barrier_semaphore()
-    each(1, n_all, lambda k: pl.semaphore_signal(
-        barrier, inc=1, device_id=flat_peer(k), device_id_type=MESH))
-    each(1, n_tp, lambda k: pl.semaphore_signal(
-        barrier, inc=1, device_id=tp_peer(k), device_id_type=MESH))
+        return g
+
+    got = {0: bring_layer(0, n_ff // 2)}
 
     def remote(src, dst, ssem, rsem, peer):
         return pltpu.make_async_remote_copy(
@@ -145,18 +150,27 @@
     sine = jnp.concatenate([jnp.sin(angles)] * (width // 128), axis=1)
     sine = jnp.where(feature < ROT // 2, -sine, sine)
 
-    columns = slots * PAGE
+    extra = cache.shape[2] - slots
+    columns = (slots + extra) * PAGE
     lanes = lane_iota((1, columns))
     col_owner = jnp.full((1, columns), -1, jnp.int32)
     home = jnp.full((slots, width), -1, jnp.int32)
     write_pos = []
     for s in range(slots):
-        limit = jnp.where(used_ref[s] == 1, fill_ref[s] + tail_ref[s], 0)
+        limit = jnp.where(used_ref[s] == 1, fill_ref[s], 0)
         here = (lanes >= s * PAGE) & (lanes < s * PAGE + limit)
         col_owner = jnp.where(here, owner_ref[s], col_owner)
         home_row = jnp.where(tail_ref[s] == 1, owner_ref[s] - my_rep * rows, -1)
         home = jnp.where(row_iota((slots, width)) == s, home_row, home)
+        new_lane = jnp.where(tail_ref[s] == 1, slots * PAGE + home_row, -1)
+        col_owner = jnp.where(lanes == new_lane, owner_ref[s], col_owner)
         write_pos.append(jnp.where(tail_ref[s] == 1, fill_ref[s], -1))
+    mask_ref[...] = jnp.where(
+        lax.rem(row_iota((heads * reqs, columns)), reqs) == col_owner, 1.0, 0.0)
+    for l in range(LAYERS):
+        for i in range(2):
+            for s in range(slots, slots + extra):
+                cache[l, i, s] = jnp.zeros((PAGE, width), bf16)
 
     head_of_lane = lane_iota((1, width)) // HD
 
@@ -172,6 +186,24 @@
     def unfold(x):
         return jnp.concatenate([x[:rows], x[rows:]], axis=1)
 
+    wide = model >= 512
+
+    def fold_c(x):
+        if wide:
+            return jnp.concatenate(
+                [x[:, c * (model // 4):(c + 1) * (model // 4)] for c in range(4)], axis=0)
+        x = jnp.concatenate([x, jnp.zeros((16 - rows, model), f32)], axis=0)
+        if model < buf_c.shape[3]:
+            x = jnp.concatenate([x, jnp.zeros((16, buf_c.shape[3] - model), f32)], axis=1)
+        return x
+
+    def unfold_c(x):
+        if wide:
+            return jnp.concatenate(
+                [x[c * rows:(c + 1) * rows] for c in range(4)], axis=1)
+        return x[0:rows, 0:model]
+
+    out_copies = []
     state = hidden_ref[...].astype(f32)
     for l in range(LAYERS):
         g = got[l]
@@ -194,9 +226,13 @@
             pl.semaphore_wait(barrier, n_all - 1 + n_tp - 1)
         each(1, n_blk, lambda k: copy_a(l)(k).start())
         for c in range(n_ff):
-            g["fc1"][c].wait()
-            buf_i[l, 0, c] = jnp.dot(lhs, wfc1[l, c], preferred_element_type=f32)
+            if g["fc1"][c] is not None:
+                g["fc1"][c].wait()
+            buf_i[l, 0, c] = jnp.dot(
+                lhs, wfc1[l, :, c * width:(c + 1) * width], preferred_element_type=f32)
         each(1, n_blk, lambda k: copy_i(l)(k).start())
+        if l + 1 < LAYERS:
+            got[l + 1] = bring_layer(l + 1, 1)
 
         each(1, n_blk, lambda k: copy_a(l)(k).wait_recv())
         mean = fold_sum(0, n_blk, lambda k, t: t + buf_a[l, k, 3, 0:rows, 0:1],
@@ -229,17 +265,10 @@
         new_k = qk[rows:]
         new_v = finish(buf_a, 2).astype(bf16).astype(f32)
 
-        for i, new in ((0, new_k), (1, new_v)):
-            fresh = jnp.zeros((slots, width), f32)
-            for r in range(rows):
-                fresh = jnp.where(home == r, new[r:r + 1], fresh)
-            fresh_ref[l, i] = fresh
-            g["cache"][i].wait()
-            for s in range(slots):
-                page = cache[l, i, s].astype(f32)
-                page = jnp.where(
-                    row_iota((PAGE, width)) == write_pos[s], fresh[s:s + 1], page)
-                cache[l, i, s] = page.astype(bf16)
+        new = (new_k, new_v)
+        for i in range(2):
+            cache[l, i, slots, 0:16] = jnp.concatenate(
+                [new[i], jnp.zeros((16 - rows, width), f32)], axis=0).astype(bf16)
 
         each(1, n_blk, lambda k: copy_i(l)(k).wait_recv())
         for c in range(n_ff):
@@ -256,11 +285,13 @@
         by_head = jnp.concatenate(
             [jnp.where(head_of_lane == h, queries, 0.0) for h in range(heads)], axis=0
         ).astype(bf16)
+        for i in range(2):
+            g["cache"][i].wait()
         keys = cache[l, 0].reshape(columns, width)
         values = cache[l, 1].reshape(columns, width)
         scores = lax.dot_general(
             by_head, keys, (((1,), (1,)), ((), ())), preferred_element_type=f32) * HD ** (-0.5)
-        mask = lax.rem(row_iota((heads * reqs, columns)), reqs) == col_owner
+        mask = mask_ref[...] > 0.0
         scores = jnp.where(mask, scores, LOWEST)
         highest = jnp.max(scores, axis=1, keepdims=True)
         weights = jnp.where(mask, jnp.exp(scores - highest), 0.0)
@@ -310,21 +341,32 @@
         g["out"][0].wait()
         branch = (
             jnp.dot(attended, wout[l], preferred_element_type=f32) + mlp_acc[...])[0:rows]
-        folded = model >= 256
-        if folded:
-            buf_c[l, 0] = fold(branch)
-        else:
-            buf_c[l, 0] = jnp.zeros(buf_c.shape[2:], f32)
-            buf_c[l, 0, 0:rows, 0:model] = branch
+        buf_c[l, 0] = fold_c(branch).astype(bf16)
         each(1, n_tp, lambda k: copy_c(l)(k).start())
+
+        for i in range(2):
+            fresh = jnp.zeros((slots, width), f32)
+            for r in range(rows):
+                fresh = jnp.where(home == r, new[i][r:r + 1], fresh)
+            for s in range(slots):
+                page = cache[l, i, s].astype(f32)
+                page = jnp.where(
+                    row_iota((PAGE, width)) == write_pos[s], fresh[s:s + 1], page)
+                cache[l, i, s] = page.astype(bf16)
+            out_copies.append(pltpu.make_async_copy(
+                cache.at[l, i, pl.ds(0, slots)], pages_ref.at[l, i], o_sem.at[l, i]))
+            out_copies[-1].start()
+
         each(1, n_tp, lambda k: copy_c(l)(k).wait_recv())
-        total = buf_c[l, lax.rem(my_tp + n_tp, n_tp)]
+        total = buf_c[l, lax.rem(my_tp + n_tp, n_tp)].astype(f32)
         for t in range(1, n_tp):
-            total = total + buf_c[l, lax.rem(my_tp - t + n_tp, n_tp)]
-        total = unfold(total) if folded else total[0:rows, 0:model]
+            total = total + buf_c[l, lax.rem(my_tp - t + n_tp, n_tp)].astype(f32)
+        total = unfold_c(total)
         state = (state + total).astype(bf16).astype(f32)
 
-    state_ref[...] = state
+    state_ref[...] = state.astype(bf16)
+    for copy in out_copies:
+        copy.wait()
     for l in range(LAYERS):
         each(1, n_blk, lambda k: copy_a(l)(k).wait_send())
         each(1, n_blk, lambda k: copy_i(l)(k).wait_send())
@@ -351,35 +393,37 @@
     n_ff = w_fc1.shape[2] // width
     n_all = n_rep * n_blk
     wq = jnp.transpose(w_qkv, (0, 2, 1, 3))
-    c_width = model // 2 if model >= 256 else 128
+    c_width = model // 4 if model >= 512 else max(model, 128)
+    extra = 128 // PAGE
     smem = pl.BlockSpec(memory_space=pltpu.SMEM)
     vmem = pl.BlockSpec(memory_space=pltpu.VMEM)
     anywhere = pl.BlockSpec(memory_space=pl.ANY)
     dma = pltpu.SemaphoreType.DMA
     n_copies = LAYERS * (3 + n_ff + 2 + 2 + 1)
-    state, fresh = pl.pallas_call(
+    return pl.pallas_call(
         functools.partial(kernel, n_rep, n_blk, n_tp),
         out_shape=(
-            jax.ShapeDtypeStruct((rows, model), f32),
-            jax.ShapeDtypeStruct((LAYERS, 2, slots, width), f32),
+            jax.ShapeDtypeStruct((rows, model), bf16),
+            jax.ShapeDtypeStruct(caches.shape, bf16),
         ),
         in_specs=[smem] * 5 + [vmem] * 3 + [anywhere] * 5,
-        out_specs=(vmem, vmem),
+        out_specs=(vmem, anywhere),
         scratch_shapes=[
             pltpu.VMEM((LAYERS, 3, model, width), bf16),
-            pltpu.VMEM((LAYERS, n_ff, model, width), bf16),
+            pltpu.VMEM((LAYERS, model, n_ff * width), bf16),
             pltpu.VMEM((LAYERS, width, model), bf16),
             pltpu.VMEM((LAYERS, 2, n_ff // 2 * width, model), bf16),
-            pltpu.VMEM((LAYERS, 2, slots, PAGE, width), bf16),
+            pltpu.VMEM((LAYERS, 2, slots + extra, PAGE, width), bf16),
             pltpu.VMEM((LAYERS, n_blk, 4, 2 * rows, width), f32),
             pltpu.VMEM((LAYERS, n_blk, n_ff, 2 * rows, width), f32),
             pltpu.VMEM((LAYERS, n_rep, 2 * rows, width // 2), f32),
             pltpu.VMEM((LAYERS, n_rep, 2 * rows, width // 2 + 128), f32),
             pltpu.VMEM((LAYERS, n_all, 2 * rows, width // 2 + 128), f32),
-            pltpu.VMEM((LAYERS, n_tp, 2 * rows, c_width), f32),
+            pltpu.VMEM((LAYERS, n_tp, 16, c_width), bf16),
             pltpu.VMEM((2 * rows, model), f32),
             pltpu.VMEM((n_ff, 2 * rows, width), bf16),
-            dma((n_copies,)),
+            pltpu.VMEM((width // HD * rows * n_rep, (slots + extra) * PAGE), f32),
+            dma((n_copies,)), dma((LAYERS, 2)),
             dma((LAYERS, n_blk)), dma((LAYERS, n_blk)),
             dma((LAYERS, n_blk)), dma((LAYERS, n_blk)),
             dma((LAYERS, n_rep)), dma((LAYERS, n_rep)),
@@ -394,11 +438,6 @@
         hidden, ln_gain, jnp.asarray(frequencies(2 * rows)),
         wq, w_fc1, w_out, w_fc2, caches,
     )
-    offsets = jnp.arange(PAGE, dtype=jnp.int32)
-    write_at = (offsets[None, :] == page_fill[:, None]) & (page_tail == 1)[:, None]
-    caches_out = jnp.where(
-        write_at[None, None, :, :, None], fresh[:, :, :, None, :].astype(bf16), caches)
-    return (state.astype(bf16), caches_out)
 
 
 def solution(mesh):

time: 39.3 us -> 37.4 us (0.952)
  other arithmetic: 4.67 us -> 0 us
  local copies, waits for them, and re-layouts: 0.01 us -> 3.6 us
  Pallas kernels: 33.7 us -> 32.9 us
    unnamed x2, local copies, waits for them, and re-layouts: 0.01 us -> 3.6 us
    convert_element_type x2 -> x0, other arithmetic: 2.16 us -> none  [the longest x1 1.32 us: per_device(): return (state.astype(bf16), caches_out)]
    select_n x1 -> x0, other arithmetic: 1.12 us -> none  [per_device(): jnp.where(write_at[None, None, :, :, None], fresh[:, :, :, None, :].astyp...]
    pallas_call x1, Pallas kernels: 33.7 us -> 32.9 us  [per_device(): pl.pallas_call(functools.partial(kernel, n_rep, n_blk, n_tp), out_shape=(...]
    and x1 -> x0, other arithmetic: 0.73 us -> none  [per_device(): (offsets[None, :] == page_fill[:, None]) & (page_tail == 1)[:, None]]
    eq x1 -> x0, other arithmetic: 0.66 us -> none  [per_device(): page_tail == 1]
where the time goes in v2:
time: 37.4 us; the launch traced here: 37.2 us
  Pallas kernels  32.9 us (88%)
  local copies, waits for them, and re-layouts  3.6 us (10%)
  between operations  0.64 us (2%)
    pallas_call x1, Pallas kernels, per_device(): pl.pallas_call(functools.partial(kernel, n_rep, n_blk, n_tp), out_shape=(...  32.9 us
    unnamed x2, local copies, waits for them, and re-layouts  3.6 us

profile of v2, /device:TPU:0, one launch (start us, length us, event | category | flops | bytes accessed | tf_op | source)
XLA Modules:
  0.0 37.2 jit_solution(5733514648750065618)
XLA Ops:
  0.6 32.9 %decode_layers.1 = (bf16[4,1024]{1,0:T(4,128)(2,1)}, bf16[2,2,8,32,512]{4,3,2,1,0:T(8,128)(2,1)}) custom-call(s32[8]{0:T(128)} %owner_ref.1, s32[8]{0:T(128)} %used_ref.1, s32[8]{0:T(128)} %fill_ref.1, s32[8]{0:T(128)} %tail_ref.1, s32[4]{0:T(128)} %pos_ref.1, bf16[4,1024]{1,0:T(4,128)(2,1)} %hidden_ref.1, f32[2,1024]{1,0:T(2,128)} %gain_ref.1, ...), custom_call_target="tpu_custom_call" | custom-call | tf_op jit(solution)/shard_map/decode_layers/pallas_call | solution.py:403
  33.6 1.3 %copy.17 = bf16[4,1024]{1,0:T(4,128)(2,1)} copy(bf16[4,1024]{1,0:T(4,128)(2,1)} %get-tuple-element.4) | data formatting | bytes 16384
  34.9 2.3 %copy.18 = bf16[2,2,8,32,512]{4,3,2,1,0:T(8,128)(2,1)} copy(bf16[2,2,8,32,512]{4,3,2,1,0:T(8,128)(2,1)} %get-tuple-element.5) | data formatting | bytes 2097152

commit v3 on v2

--- a/solution.py
+++ b/solution.py
@@ -47,9 +47,9 @@
     owner_ref, used_ref, fill_ref, tail_ref, pos_ref,
     hidden_ref, gain_ref, freq_ref,
     wqkv_hbm, wfc1_hbm, wout_hbm, wfc2_hbm, cache_hbm,
-    state_ref, pages_ref,
+    state_ref, fresh_ref, bound_hbm,
     wqkv, wfc1, wout, wfc2, cache,
-    buf_a, buf_i, buf_q, msg, buf_b, buf_c, mlp_acc, act_ref, mask_ref,
+    buf_a, buf_i, buf_q, msg, buf_b, buf_c, mlp_acc, act_ref, mask_ref, bound_ref,
     w_sem, o_sem, a_send, a_recv, i_send, i_recv, q_send, q_recv, b_send, b_recv, c_send, c_recv,
 ):
     f32, bf16 = jnp.float32, jnp.bfloat16
@@ -61,7 +61,7 @@
     n_ff = wfc1.shape[2] // width
     reqs = rows * n_rep
     n_all = n_rep * n_blk
-    half = width // 2
+    quarter = width // 4
     my_rep, my_blk, my_tp = lax.axis_index("rep"), lax.axis_index("blk"), lax.axis_index("tp")
     my_flat = my_rep * n_blk + my_blk
     ff_half = n_ff // 2
@@ -118,9 +118,11 @@
             src_ref=src, dst_ref=dst, send_sem=ssem, recv_sem=rsem,
             device_id=peer, device_id_type=MESH)
 
-    def copy_a(l):
+    def copy_a(l, part):
+        piece = pl.ds(2 * part, 2)
         return lambda k: remote(
-            buf_a.at[l, 0], buf_a.at[l, k], a_send.at[l, k], a_recv.at[l, k], blk_peer(k))
+            buf_a.at[l, 0, piece], buf_a.at[l, k, piece],
+            a_send.at[l, k, part], a_recv.at[l, k, part], blk_peer(k))
 
     def copy_i(l):
         return lambda k: remote(
@@ -155,7 +157,6 @@
     lanes = lane_iota((1, columns))
     col_owner = jnp.full((1, columns), -1, jnp.int32)
     home = jnp.full((slots, width), -1, jnp.int32)
-    write_pos = []
     for s in range(slots):
         limit = jnp.where(used_ref[s] == 1, fill_ref[s], 0)
         here = (lanes >= s * PAGE) & (lanes < s * PAGE + limit)
@@ -164,7 +165,11 @@
         home = jnp.where(row_iota((slots, width)) == s, home_row, home)
         new_lane = jnp.where(tail_ref[s] == 1, slots * PAGE + home_row, -1)
         col_owner = jnp.where(lanes == new_lane, owner_ref[s], col_owner)
-        write_pos.append(jnp.where(tail_ref[s] == 1, fill_ref[s], -1))
+        write_pos = jnp.where(tail_ref[s] == 1, fill_ref[s], -1)
+        bound_ref[s] = jnp.where(
+            row_iota((PAGE, width)) == write_pos, -jnp.inf, jnp.inf).astype(bf16)
+    bound_copy = pltpu.make_async_copy(bound_ref, bound_hbm, o_sem.at[0])
+    bound_copy.start()
     mask_ref[...] = jnp.where(
         lax.rem(row_iota((heads * reqs, columns)), reqs) == col_owner, 1.0, 0.0)
     for l in range(LAYERS):
@@ -181,17 +186,22 @@
         return out
 
     def fold(x):
-        return jnp.concatenate([x[:, :x.shape[1] // 2], x[:, x.shape[1] // 2:]], axis=0)
+        part = x.shape[1] // 4
+        return jnp.concatenate([x[:, c * part:(c + 1) * part] for c in range(4)], axis=0)
 
     def unfold(x):
-        return jnp.concatenate([x[:rows], x[rows:]], axis=1)
+        x = x.astype(f32)
+        return jnp.concatenate([x[c * rows:(c + 1) * rows] for c in range(4)], axis=1)
+
+    def split(x):
+        high = x.astype(bf16).astype(f32)
+        return high, (x - high).astype(bf16).astype(f32)
 
     wide = model >= 512
 
     def fold_c(x):
         if wide:
-            return jnp.concatenate(
-                [x[:, c * (model // 4):(c + 1) * (model // 4)] for c in range(4)], axis=0)
+            return fold(x)
         x = jnp.concatenate([x, jnp.zeros((16 - rows, model), f32)], axis=0)
         if model < buf_c.shape[3]:
             x = jnp.concatenate([x, jnp.zeros((16, buf_c.shape[3] - model), f32)], axis=1)
@@ -199,11 +209,9 @@
 
     def unfold_c(x):
         if wide:
-            return jnp.concatenate(
-                [x[c * rows:(c + 1) * rows] for c in range(4)], axis=1)
+            return unfold(x)
         return x[0:rows, 0:model]
 
-    out_copies = []
     state = hidden_ref[...].astype(f32)
     for l in range(LAYERS):
         g = got[l]
@@ -218,53 +226,67 @@
             axis=0).astype(bf16)
         stat_lane = lane_iota((rows, width))
         stats = jnp.where(stat_lane < 128, own_mean, own_square)
-        buf_a[l, 0, 3] = jnp.concatenate([stats, jnp.zeros((rows, width), f32)], axis=0)
-        for j in range(3):
+        buf_a[l, 0, 0] = jnp.concatenate([stats, jnp.zeros((rows, width), f32)], axis=0)
+
+        def project(j):
             g["qkv"][j].wait()
-            buf_a[l, 0, j] = jnp.dot(lhs, wqkv[l, j], preferred_element_type=f32)
-        if l == 0:
-            pl.semaphore_wait(barrier, n_all - 1 + n_tp - 1)
-        each(1, n_blk, lambda k: copy_a(l)(k).start())
-        for c in range(n_ff):
+            buf_a[l, 0, 1 + j] = jnp.dot(lhs, wqkv[l, j], preferred_element_type=f32)
+
+        def project_ff(c):
             if g["fc1"][c] is not None:
                 g["fc1"][c].wait()
             buf_i[l, 0, c] = jnp.dot(
                 lhs, wfc1[l, :, c * width:(c + 1) * width], preferred_element_type=f32)
+
+        project(0)
+        if l == 0:
+            pl.semaphore_wait(barrier, n_all - 1 + n_tp - 1)
+        each(1, n_blk, lambda k: copy_a(l, 0)(k).start())
+        project(1)
+        project(2)
+        each(1, n_blk, lambda k: copy_a(l, 1)(k).start())
+        for c in range(ff_half):
+            project_ff(c)
+
+        each(1, n_blk, lambda k: copy_a(l, 0)(k).wait_recv())
+        mean = fold_sum(0, n_blk, lambda k, t: t + buf_a[l, k, 0, 0:rows, 0:1],
+                        jnp.zeros((rows, 1), f32)) / n_blk
+
+        def add_square(k, total):
+            off = buf_a[l, k, 0, 0:rows, 0:1] - mean
+            return total + (buf_a[l, k, 0, 0:rows, 128:129] + model * (off * off))
+
+        square = fold_sum(0, n_blk, add_square, jnp.zeros((rows, 1), f32))
+        scale = lax.rsqrt(square / full_model + EPSILON)
+
+        def finish(buf, j):
+            def add(k, total):
+                off = buf_a[l, k, 0, 0:rows, 0:1] - mean
+                block = buf[l, k, j]
+                gained = block[rows:rows + 1] + block[rows + 1:rows + 2]
+                return total + (block[0:rows] + off * gained)
+
+            return fold_sum(0, n_blk, add, jnp.zeros((rows, width), f32)) * scale
+
+        def rotate(x):
+            turned = jnp.where(
+                feature < ROT // 2,
+                pltpu.roll(x, width - ROT // 2, 1),
+                pltpu.roll(x, ROT // 2, 1))
+            return (x * cosine + turned * sine).astype(bf16).astype(f32)
+
+        blank = jnp.zeros((rows, width), f32)
+        own_queries = rotate(jnp.concatenate([finish(buf_a, 1), blank], axis=0))[:rows]
+        buf_q[l, 0] = fold(own_queries).astype(bf16)
+        each(1, n_rep, lambda k: copy_q(l)(k).start())
+        for c in range(ff_half, n_ff):
+            project_ff(c)
         each(1, n_blk, lambda k: copy_i(l)(k).start())
         if l + 1 < LAYERS:
             got[l + 1] = bring_layer(l + 1, 1)
-
-        each(1, n_blk, lambda k: copy_a(l)(k).wait_recv())
-        mean = fold_sum(0, n_blk, lambda k, t: t + buf_a[l, k, 3, 0:rows, 0:1],
-                        jnp.zeros((rows, 1), f32)) / n_blk
-
-        def add_square(k, total):
-            off = buf_a[l, k, 3, 0:rows, 0:1] - mean
-            return total + (buf_a[l, k, 3, 0:rows, 128:129] + model * (off * off))
-
-        square = fold_sum(0, n_blk, add_square, jnp.zeros((rows, 1), f32))
-        scale = lax.rsqrt(square / full_model + EPSILON)
-
-        def finish(buf, j):
-            def add(k, total):
-                off = buf_a[l, k, 3, 0:rows, 0:1] - mean
-                block = buf[l, k, j]
-                gained = block[rows:rows + 1] + block[rows + 1:rows + 2]
-                return total + (block[0:rows] + off * gained)
-
-            return fold_sum(0, n_blk, add, jnp.zeros((rows, width), f32)) * scale
-
-        qk = jnp.concatenate([finish(buf_a, 0), finish(buf_a, 1)], axis=0)
-        turned = jnp.where(
-            feature < ROT // 2,
-            pltpu.roll(qk, width - ROT // 2, 1),
-            pltpu.roll(qk, ROT // 2, 1))
-        qk = (qk * cosine + turned * sine).astype(bf16).astype(f32)
-        buf_q[l, 0] = fold(qk[:rows])
-        each(1, n_rep, lambda k: copy_q(l)(k).start())
-        new_k = qk[rows:]
-        new_v = finish(buf_a, 2).astype(bf16).astype(f32)
-
+        each(1, n_blk, lambda k: copy_a(l, 1)(k).wait_recv())
+        new_k = rotate(jnp.concatenate([finish(buf_a, 2), blank], axis=0))[:rows]
+        new_v = finish(buf_a, 3).astype(bf16).astype(f32)
         new = (new_k, new_v)
         for i in range(2):
             cache[l, i, slots, 0:16] = jnp.concatenate(
@@ -293,25 +315,26 @@
             by_head, keys, (((1,), (1,)), ((), ())), preferred_element_type=f32) * HD ** (-0.5)
         mask = mask_ref[...] > 0.0
         scores = jnp.where(mask, scores, LOWEST)
-        highest = jnp.max(scores, axis=1, keepdims=True)
+        high_pieces = split(jnp.max(scores, axis=1, keepdims=True))
+        highest = high_pieces[0] + high_pieces[1]
         weights = jnp.where(mask, jnp.exp(scores - highest), 0.0)
         totals = jnp.sum(weights, axis=1, keepdims=True)
         spread = jnp.dot(weights.astype(bf16), values, preferred_element_type=f32)
         out = spread[0:reqs]
         stat_shape = (reqs, 128)
-        high_stat = jnp.zeros(stat_shape, f32)
-        total_stat = jnp.ones(stat_shape, f32)
+        stats = [jnp.zeros(stat_shape, f32), jnp.zeros(stat_shape, f32),
+                 jnp.ones(stat_shape, f32), jnp.zeros(stat_shape, f32)]
         for h in range(heads):
             part = slice(h * reqs, (h + 1) * reqs)
             if h > 0:
                 out = jnp.where(head_of_lane == h, spread[part], out)
-            high_stat = jnp.where(lane_iota(stat_shape) == h, highest[part], high_stat)
-            total_stat = jnp.where(lane_iota(stat_shape) == h, totals[part], total_stat)
+            for i, piece in enumerate(high_pieces + split(totals)):
+                stats[i] = jnp.where(lane_iota(stat_shape) == h, piece[part], stats[i])
         for r in range(n_rep):
             part = slice(r * rows, (r + 1) * rows)
-            msg[l, r, :, 0:half] = fold(out[part])
-            msg[l, r, :, half:half + 128] = jnp.concatenate(
-                [high_stat[part], total_stat[part]], axis=0)
+            msg[l, r] = jnp.concatenate(
+                [fold(out[part]), jnp.concatenate([stat[part] for stat in stats], axis=0)],
+                axis=1).astype(bf16)
         each(1, n_all, lambda k: copy_b(l)(k).start())
         buf_b[l, 0] = msg[l, my_rep]
 
@@ -321,16 +344,20 @@
             wfc2[l, 1], preferred_element_type=f32)
 
         each(1, n_all, lambda k: copy_b(l)(k).wait_recv())
+
+        def stat_of(k, first):
+            stat = buf_b[l, k, :, quarter:quarter + 128].astype(f32)
+            return stat[first * rows:(first + 1) * rows] + stat[(first + 1) * rows:(first + 2) * rows]
+
         top = fold_sum(
-            0, n_all,
-            lambda k, t: jnp.maximum(t, buf_b[l, k, 0:rows, half:half + 128]),
+            0, n_all, lambda k, t: jnp.maximum(t, stat_of(k, 0)),
             jnp.full((rows, 128), LOWEST, f32))
 
         def merge(k, carry):
             denom, numer = carry
-            factor = jnp.exp(buf_b[l, k, 0:rows, half:half + 128] - top)
-            denom = denom + factor * buf_b[l, k, rows:2 * rows, half:half + 128]
-            numer = numer + expand(factor) * unfold(buf_b[l, k, :, 0:half])
+            factor = jnp.exp(stat_of(k, 0) - top)
+            denom = denom + factor * stat_of(k, 2)
+            numer = numer + expand(factor) * unfold(buf_b[l, k, :, 0:quarter])
             return denom, numer
 
         denom, numer = fold_sum(
@@ -348,14 +375,7 @@
             fresh = jnp.zeros((slots, width), f32)
             for r in range(rows):
                 fresh = jnp.where(home == r, new[i][r:r + 1], fresh)
-            for s in range(slots):
-                page = cache[l, i, s].astype(f32)
-                page = jnp.where(
-                    row_iota((PAGE, width)) == write_pos[s], fresh[s:s + 1], page)
-                cache[l, i, s] = page.astype(bf16)
-            out_copies.append(pltpu.make_async_copy(
-                cache.at[l, i, pl.ds(0, slots)], pages_ref.at[l, i], o_sem.at[l, i]))
-            out_copies[-1].start()
+            fresh_ref[l, i] = fresh.astype(bf16)
 
         each(1, n_tp, lambda k: copy_c(l)(k).wait_recv())
         total = buf_c[l, lax.rem(my_tp + n_tp, n_tp)].astype(f32)
@@ -364,11 +384,11 @@
         total = unfold_c(total)
         state = (state + total).astype(bf16).astype(f32)
 
-    state_ref[...] = state.astype(bf16)
-    for copy in out_copies:
-        copy.wait()
+    state_ref[...] = state
+    bound_copy.wait()
     for l in range(LAYERS):
-        each(1, n_blk, lambda k: copy_a(l)(k).wait_send())
+        each(1, n_blk, lambda k: copy_a(l, 0)(k).wait_send())
+        each(1, n_blk, lambda k: copy_a(l, 1)(k).wait_send())
         each(1, n_blk, lambda k: copy_i(l)(k).wait_send())
         each(1, n_rep, lambda k: copy_q(l)(k).wait_send())
         each(1, n_all, lambda k: copy_b(l)(k).wait_send())
@@ -400,14 +420,15 @@
     anywhere = pl.BlockSpec(memory_space=pl.ANY)
     dma = pltpu.SemaphoreType.DMA
     n_copies = LAYERS * (3 + n_ff + 2 + 2 + 1)
-    return pl.pallas_call(
+    state, fresh, bound = pl.pallas_call(
         functools.partial(kernel, n_rep, n_blk, n_tp),
         out_shape=(
-            jax.ShapeDtypeStruct((rows, model), bf16),
-            jax.ShapeDtypeStruct(caches.shape, bf16),
+            jax.ShapeDtypeStruct((rows, model), f32),
+            jax.ShapeDtypeStruct((LAYERS, 2, slots, width), bf16),
+            jax.ShapeDtypeStruct((slots, PAGE, width), bf16),
         ),
         in_specs=[smem] * 5 + [vmem] * 3 + [anywhere] * 5,
-        out_specs=(vmem, anywhere),
+        out_specs=(vmem, vmem, anywhere),
         scratch_shapes=[
             pltpu.VMEM((LAYERS, 3, model, width), bf16),
             pltpu.VMEM((LAYERS, model, n_ff * width), bf16),
@@ -416,15 +437,16 @@
             pltpu.VMEM((LAYERS, 2, slots + extra, PAGE, width), bf16),
             pltpu.VMEM((LAYERS, n_blk, 4, 2 * rows, width), f32),
             pltpu.VMEM((LAYERS, n_blk, n_ff, 2 * rows, width), f32),
-            pltpu.VMEM((LAYERS, n_rep, 2 * rows, width // 2), f32),
-            pltpu.VMEM((LAYERS, n_rep, 2 * rows, width // 2 + 128), f32),
-            pltpu.VMEM((LAYERS, n_all, 2 * rows, width // 2 + 128), f32),
+            pltpu.VMEM((LAYERS, n_rep, 4 * rows, width // 4), bf16),
+            pltpu.VMEM((LAYERS, n_rep, 4 * rows, width // 4 + 128), bf16),
+            pltpu.VMEM((LAYERS, n_all, 4 * rows, width // 4 + 128), bf16),
             pltpu.VMEM((LAYERS, n_tp, 16, c_width), bf16),
             pltpu.VMEM((2 * rows, model), f32),
             pltpu.VMEM((n_ff, 2 * rows, width), bf16),
             pltpu.VMEM((width // HD * rows * n_rep, (slots + extra) * PAGE), f32),
-            dma((n_copies,)), dma((LAYERS, 2)),
-            dma((LAYERS, n_blk)), dma((LAYERS, n_blk)),
+            pltpu.VMEM((slots, PAGE, width), bf16),
+            dma((n_copies,)), dma((1,)),
+            dma((LAYERS, n_blk, 2)), dma((LAYERS, n_blk, 2)),
             dma((LAYERS, n_blk)), dma((LAYERS, n_blk)),
             dma((LAYERS, n_rep)), dma((LAYERS, n_rep)),
             dma((LAYERS, n_all)), dma((LAYERS, n_all)),
@@ -438,6 +460,8 @@
         hidden, ln_gain, jnp.asarray(frequencies(2 * rows)),
         wq, w_fc1, w_out, w_fc2, caches,
     )
+    caches_out = jnp.where(caches < bound[None, None], caches, fresh[:, :, :, None, :])
+    return (state.astype(bf16), caches_out)
 
 
 def solution(mesh):

time: 37.4 us -> 36.7 us (0.981)
  local copies, waits for them, and re-layouts: 3.6 us -> 0.01 us
  other arithmetic: 0 us -> 3.38 us
  Pallas kernels: 32.9 us -> 32.4 us
    unnamed x2, local copies, waits for them, and re-layouts: 3.6 us -> 0.01 us
    select_n x0 -> x1, other arithmetic: none -> 2.06 us  [per_device(): jnp.where(caches < bound[None, None], caches, fresh[:, :, :, None, :])]
    convert_element_type x0 -> x1, other arithmetic: none -> 1.32 us  [per_device(): return (state.astype(bf16), caches_out)]
    pallas_call x1, Pallas kernels: 32.9 us -> 32.4 us  [per_device(): pl.pallas_call(functools.partial(kernel, n_rep, n_blk, n_tp), out_shape=(...]
where the time goes in v3:
time: 36.7 us; the launch traced here: 36.4 us
  Pallas kernels  32.4 us (88%)
  other arithmetic  3.38 us (9%)
  between operations  0.65 us (2%)
    pallas_call x1, Pallas kernels, per_device(): pl.pallas_call(functools.partial(kernel, n_rep, n_blk, n_tp), out_shape=(...  32.4 us
    select_n x1, other arithmetic, per_device(): jnp.where(caches < bound[None, None], caches, fresh[:, :, :, None, :])  2.06 us
    convert_element_type x1, other arithmetic, per_device(): return (state.astype(bf16), caches_out)  1.32 us

profile of v3, /device:TPU:0, one launch (start us, length us, event | category | flops | bytes accessed | tf_op | source)
XLA Modules:
  0.0 36.4 jit_solution(6440114803710240611)
XLA Ops:
  0.6 0.0 copy-start
  0.6 32.4 %decode_layers.1 = (f32[4,1024]{1,0:T(4,128)}, bf16[2,2,8,512]{3,2,1,0:T(8,128)(2,1)}, bf16[8,32,512]{2,1,0:T(8,128)(2,1)}) custom-call(s32[8]{0:T(128)} %owner_ref.1, s32[8]{0:T(128)} %used_ref.1, s32[8]{0:T(128)} %fill_ref.1, s32[8]{0:T(128)} %tail_ref.1, s32[4]{0:T(128)} %pos_ref.1, bf16[4,1024]{1,0:T(4,128)(2,1)} %hidden_ref.1, f32[2,1024]{1,0:T(2,128)} %gain_ref.1, ...), custom_call_target="tpu_custom_call" | custom-call | tf_op jit(solution)/shard_map/decode_layers/pallas_call | solution.py:423
  33.0 1.3 %convert_element_type.3 = bf16[4,1024]{1,0:T(4,128)(2,1)} convert(f32[4,1024]{1,0:T(4,128)} %get-tuple-element.5) | non-fusion elementwise | flops 4096 | bytes 24576 | tf_op jit(solution)/shard_map/convert_element_type | solution.py:464
  34.4 0.0 copy-done
  34.4 2.1 %compare_select_fusion = bf16[2,2,8,32,512]{4,3,2,1,0:T(8,128)(2,1)} fusion(bf16[2,2,8,32,512]{4,3,2,1,0:T(8,128)(2,1)S(1)} %copy-done, bf16[2,2,8,512]{3,2,1,0:T(8,128)(2,1)} %get-tuple-element.7, bf16[8,32,512]{2,1,0:T(8,128)(2,1)} %get-tuple-element.6), kind=kLoop, calls=%fused_computation | loop fusion | flops 1048576 | bytes 2392064 | tf_op jit(solution)/shard_map/jit(_where)/select_n | solution.py:463
Async XLA Ops:
  0.6 33.7 %copy-start = (bf16[2,2,8,32,512]{4,3,2,1,0:T(8,128)(2,1)S(1)}, bf16[2,2,8,32,512]{4,3,2,1,0:T(8,128)(2,1)}, u32[]{:S(2)}) copy-start(bf16[2,2,8,32,512]{4,3,2,1,0:T(8,128)(2,1)} %cache_hbm.1) | copy-start | bytes 3145732

commit v4 on v3

--- a/solution.py
+++ b/solution.py
@@ -49,8 +49,9 @@
     wqkv_hbm, wfc1_hbm, wout_hbm, wfc2_hbm, cache_hbm,
     state_ref, fresh_ref, bound_hbm,
     wqkv, wfc1, wout, wfc2, cache,
-    buf_a, buf_i, buf_q, msg, buf_b, buf_c, mlp_acc, act_ref, mask_ref, bound_ref,
+    buf_a, buf_i, buf_q, msg, buf_b, buf_c, buf_x, msg_m, buf_m, mask_ref, bound_ref,
     w_sem, o_sem, a_send, a_recv, i_send, i_recv, q_send, q_recv, b_send, b_recv, c_send, c_recv,
+    x_send, x_recv, m_send, m_recv,
 ):
     f32, bf16 = jnp.float32, jnp.bfloat16
     rows, model = hidden_ref.shape
@@ -58,13 +59,13 @@
     slots = owner_ref.shape[0]
     width = wout.shape[1]
     heads = width // HD
-    n_ff = wfc1.shape[2] // width
+    ff = wfc1.shape[2]
     reqs = rows * n_rep
     n_all = n_rep * n_blk
     quarter = width // 4
     my_rep, my_blk, my_tp = lax.axis_index("rep"), lax.axis_index("blk"), lax.axis_index("tp")
     my_flat = my_rep * n_blk + my_blk
-    ff_half = n_ff // 2
+    ff_at = pl.multiple_of(my_rep * ff, ff)
 
     def flat_peer(k):
         to = lax.rem(my_flat + k, n_all)
@@ -93,25 +94,17 @@
         local.append(copy)
         return copy
 
-    def bring_layer(l, pieces):
+    def bring_layer(l):
         g = {}
         g["qkv"] = [bring(wqkv_hbm.at[l, j], wqkv.at[l, j]) for j in range(3)]
-        step = n_ff // pieces
-        g["fc1"] = [
-            bring(wfc1_hbm.at[l, :, pl.ds(c * width, step * width)],
-                  wfc1.at[l, :, pl.ds(c * width, step * width)])
-            if c % step == 0 else None for c in range(n_ff)
-        ]
+        g["fc1"] = [bring(wfc1_hbm.at[l, :, pl.ds(ff_at, ff)], wfc1.at[l])]
         g["cache"] = [
             bring(cache_hbm.at[l, i], cache.at[l, i, pl.ds(0, slots)]) for i in range(2)]
-        g["fc2"] = [
-            bring(wfc2_hbm.at[l, pl.ds(i * ff_half * width, ff_half * width), :], wfc2.at[l, i])
-            for i in range(2)
-        ]
+        g["fc2"] = [bring(wfc2_hbm.at[l, pl.ds(ff_at, ff), :], wfc2.at[l])]
         g["out"] = [bring(wout_hbm.at[l], wout.at[l])]
         return g
 
-    got = {0: bring_layer(0, n_ff // 2)}
+    got = {0: bring_layer(0)}
 
     def remote(src, dst, ssem, rsem, peer):
         return pltpu.make_async_remote_copy(
@@ -136,6 +129,15 @@
         return lambda k: remote(
             msg.at[l, lax.rem(my_flat + k, n_all) // n_blk], buf_b.at[l, k],
             b_send.at[l, k], b_recv.at[l, k], flat_peer(k))
+
+    def copy_x(l):
+        return lambda k: remote(
+            buf_x.at[l, 0], buf_x.at[l, k], x_send.at[l, k], x_recv.at[l, k], rep_peer(k))
+
+    def copy_m(l):
+        return lambda k: remote(
+            msg_m.at[l, lax.rem(my_rep + k, n_rep)], buf_m.at[l, k],
+            m_send.at[l, k], m_recv.at[l, k], rep_peer(k))
 
     def copy_c(l):
         return lambda k: remote(
@@ -212,12 +214,51 @@
             return unfold(x)
         return x[0:rows, 0:model]
 
+    def fold_m(x):
+        if wide:
+            return jnp.concatenate([x[:, :model // 2], x[:, model // 2:]], axis=0)
+        x = jnp.concatenate([x, jnp.zeros((2 * rows - rows, model), f32)], axis=0)
+        if model < buf_m.shape[3]:
+            x = jnp.concatenate(
+                [x, jnp.zeros((2 * rows, buf_m.shape[3] - model), f32)], axis=1)
+        return x
+
+    def unfold_m(x):
+        if wide:
+            return jnp.concatenate([x[:rows], x[rows:]], axis=1)
+        return x[0:rows, 0:model]
+
+    def center(x):
+        own_mean = jnp.sum(x, axis=1, keepdims=True) / model
+        centered = x - own_mean
+        return own_mean, centered, jnp.sum(centered * centered, axis=1, keepdims=True)
+
+    def whole_norm(mean_of, square_of, count):
+        blank = jnp.zeros((count, 1), f32)
+        mean = fold_sum(0, n_blk, lambda k, t: t + mean_of(k), blank) / n_blk
+
+        def add_square(k, total):
+            off = mean_of(k) - mean
+            return total + (square_of(k) + model * (off * off))
+
+        square = fold_sum(0, n_blk, add_square, blank)
+        return mean, lax.rsqrt(square / full_model + EPSILON)
+
+    def sum_parts(block_of, mean_of, mean, scale, count, columns):
+        def add(k, total):
+            block = block_of(k)
+            gained = block[count:count + 1] + block[count + 1:count + 2]
+            return total + (block[0:count] + (mean_of(k) - mean) * gained)
+
+        return fold_sum(0, n_blk, add, jnp.zeros((count, columns), f32)) * scale
+
     state = hidden_ref[...].astype(f32)
     for l in range(LAYERS):
         g = got[l]
-        own_mean = jnp.sum(state, axis=1, keepdims=True) / model
-        centered = state - own_mean
-        own_square = jnp.sum(centered * centered, axis=1, keepdims=True)
+        buf_x[l, 0] = fold_c(state).astype(bf16)
+        if l > 0:
+            each(1, n_rep, lambda k: copy_x(l)(k).start())
+        own_mean, centered, own_square = center(state)
         gain = gain_ref[l:l + 1, :]
         gain_hi = gain.astype(bf16).astype(f32)
         gain_lo = gain - gain_hi
@@ -232,41 +273,23 @@
             g["qkv"][j].wait()
             buf_a[l, 0, 1 + j] = jnp.dot(lhs, wqkv[l, j], preferred_element_type=f32)
 
-        def project_ff(c):
-            if g["fc1"][c] is not None:
-                g["fc1"][c].wait()
-            buf_i[l, 0, c] = jnp.dot(
-                lhs, wfc1[l, :, c * width:(c + 1) * width], preferred_element_type=f32)
-
         project(0)
         if l == 0:
             pl.semaphore_wait(barrier, n_all - 1 + n_tp - 1)
+            each(1, n_rep, lambda k: copy_x(l)(k).start())
         each(1, n_blk, lambda k: copy_a(l, 0)(k).start())
         project(1)
         project(2)
         each(1, n_blk, lambda k: copy_a(l, 1)(k).start())
-        for c in range(ff_half):
-            project_ff(c)
-
         each(1, n_blk, lambda k: copy_a(l, 0)(k).wait_recv())
-        mean = fold_sum(0, n_blk, lambda k, t: t + buf_a[l, k, 0, 0:rows, 0:1],
-                        jnp.zeros((rows, 1), f32)) / n_blk
-
-        def add_square(k, total):
-            off = buf_a[l, k, 0, 0:rows, 0:1] - mean
-            return total + (buf_a[l, k, 0, 0:rows, 128:129] + model * (off * off))
-
-        square = fold_sum(0, n_blk, add_square, jnp.zeros((rows, 1), f32))
-        scale = lax.rsqrt(square / full_model + EPSILON)
-
-        def finish(buf, j):
-            def add(k, total):
-                off = buf_a[l, k, 0, 0:rows, 0:1] - mean
-                block = buf[l, k, j]
-                gained = block[rows:rows + 1] + block[rows + 1:rows + 2]
-                return total + (block[0:rows] + off * gained)
-
-            return fold_sum(0, n_blk, add, jnp.zeros((rows, width), f32)) * scale
+        def mean_a(k):
+            return buf_a[l, k, 0, 0:rows, 0:1]
+
+        mean, scale = whole_norm(
+            mean_a, lambda k: buf_a[l, k, 0, 0:rows, 128:129], rows)
+
+        def finish(j):
+            return sum_parts(lambda k: buf_a[l, k, j], mean_a, mean, scale, rows, width)
 
         def rotate(x):
             turned = jnp.where(
@@ -276,30 +299,48 @@
             return (x * cosine + turned * sine).astype(bf16).astype(f32)
 
         blank = jnp.zeros((rows, width), f32)
-        own_queries = rotate(jnp.concatenate([finish(buf_a, 1), blank], axis=0))[:rows]
+        own_queries = rotate(jnp.concatenate([finish(1), blank], axis=0))[:rows]
         buf_q[l, 0] = fold(own_queries).astype(bf16)
         each(1, n_rep, lambda k: copy_q(l)(k).start())
-        for c in range(ff_half, n_ff):
-            project_ff(c)
+
+        each(1, n_rep, lambda k: copy_x(l)(k).wait_recv())
+        all_state = jnp.concatenate(
+            [unfold_c(buf_x[l, lax.rem(my_rep - t + n_rep, n_rep)].astype(f32))
+             for t in range(n_rep)], axis=0)
+        all_mean, all_centered, all_square = center(all_state)
+        all_lhs = jnp.concatenate(
+            [all_centered * gain, gain_hi, gain_lo, jnp.zeros((6, model), f32)],
+            axis=0).astype(bf16)
+        all_stats = jnp.where(lane_iota((reqs, 128)) < 64, all_mean, all_square)
+        buf_i[l, 0, :, ff:ff + 128] = jnp.concatenate(
+            [all_stats, jnp.zeros((8, 128), f32)], axis=0)
+        g["fc1"][0].wait()
+        buf_i[l, 0, :, 0:ff] = jnp.dot(all_lhs, wfc1[l], preferred_element_type=f32)
         each(1, n_blk, lambda k: copy_i(l)(k).start())
         if l + 1 < LAYERS:
-            got[l + 1] = bring_layer(l + 1, 1)
+            got[l + 1] = bring_layer(l + 1)
         each(1, n_blk, lambda k: copy_a(l, 1)(k).wait_recv())
-        new_k = rotate(jnp.concatenate([finish(buf_a, 2), blank], axis=0))[:rows]
-        new_v = finish(buf_a, 3).astype(bf16).astype(f32)
+        new_k = rotate(jnp.concatenate([finish(2), blank], axis=0))[:rows]
+        new_v = finish(3).astype(bf16).astype(f32)
         new = (new_k, new_v)
         for i in range(2):
             cache[l, i, slots, 0:16] = jnp.concatenate(
                 [new[i], jnp.zeros((16 - rows, width), f32)], axis=0).astype(bf16)
 
         each(1, n_blk, lambda k: copy_i(l)(k).wait_recv())
-        for c in range(n_ff):
-            act = jax.nn.gelu(finish(buf_i, c), approximate=True)
-            act_ref[c] = jnp.concatenate([act, jnp.zeros((rows, width), f32)], axis=0).astype(bf16)
+
+        def mean_i(k):
+            return buf_i[l, k, 0:reqs, ff:ff + 1]
+
+        mean, scale = whole_norm(
+            mean_i, lambda k: buf_i[l, k, 0:reqs, ff + 64:ff + 65], reqs)
+        inner = sum_parts(lambda k: buf_i[l, k, :, 0:ff], mean_i, mean, scale, reqs, ff)
+        act = jax.nn.gelu(inner, approximate=True).astype(bf16)
         g["fc2"][0].wait()
-        mlp_acc[...] = jnp.dot(
-            jnp.concatenate([act_ref[c] for c in range(ff_half)], axis=1),
-            wfc2[l, 0], preferred_element_type=f32)
+        mlp_all = jnp.dot(act, wfc2[l], preferred_element_type=f32)
+        for r in range(n_rep):
+            msg_m[l, r] = fold_m(mlp_all[r * rows:(r + 1) * rows])
+        each(1, n_rep, lambda k: copy_m(l)(k).start())
 
         each(1, n_rep, lambda k: copy_q(l)(k).wait_recv())
         queries = jnp.concatenate(
@@ -338,10 +379,8 @@
         each(1, n_all, lambda k: copy_b(l)(k).start())
         buf_b[l, 0] = msg[l, my_rep]
 
-        g["fc2"][1].wait()
-        mlp_acc[...] += jnp.dot(
-            jnp.concatenate([act_ref[c] for c in range(ff_half, n_ff)], axis=1),
-            wfc2[l, 1], preferred_element_type=f32)
+        each(1, n_rep, lambda k: copy_m(l)(k).wait_recv())
+        mlp = fold_sum(1, n_rep, lambda k, t: t + buf_m[l, k], msg_m[l, my_rep])
 
         each(1, n_all, lambda k: copy_b(l)(k).wait_recv())
 
@@ -367,7 +406,7 @@
             [attended, jnp.zeros((rows, width), f32)], axis=0).astype(bf16)
         g["out"][0].wait()
         branch = (
-            jnp.dot(attended, wout[l], preferred_element_type=f32) + mlp_acc[...])[0:rows]
+            jnp.dot(attended, wout[l], preferred_element_type=f32)[0:rows] + unfold_m(mlp))
         buf_c[l, 0] = fold_c(branch).astype(bf16)
         each(1, n_tp, lambda k: copy_c(l)(k).start())
 
@@ -391,6 +430,8 @@
         each(1, n_blk, lambda k: copy_a(l, 1)(k).wait_send())
         each(1, n_blk, lambda k: copy_i(l)(k).wait_send())
         each(1, n_rep, lambda k: copy_q(l)(k).wait_send())
+        each(1, n_rep, lambda k: copy_x(l)(k).wait_send())
+        each(1, n_rep, lambda k: copy_m(l)(k).wait_send())
         each(1, n_all, lambda k: copy_b(l)(k).wait_send())
         each(1, n_tp, lambda k: copy_c(l)(k).wait_send())
 
@@ -410,16 +451,17 @@
     rows, model = hidden.shape
     slots = page_owner.shape[0]
     width = w_out.shape[1]
-    n_ff = w_fc1.shape[2] // width
+    ff = w_fc1.shape[2] // n_rep
     n_all = n_rep * n_blk
     wq = jnp.transpose(w_qkv, (0, 2, 1, 3))
     c_width = model // 4 if model >= 512 else max(model, 128)
+    m_width = model // 2 if model >= 512 else max(model, 128)
     extra = 128 // PAGE
     smem = pl.BlockSpec(memory_space=pltpu.SMEM)
     vmem = pl.BlockSpec(memory_space=pltpu.VMEM)
     anywhere = pl.BlockSpec(memory_space=pl.ANY)
     dma = pltpu.SemaphoreType.DMA
-    n_copies = LAYERS * (3 + n_ff + 2 + 2 + 1)
+    n_copies = LAYERS * (3 + 1 + 2 + 1 + 1)
     state, fresh, bound = pl.pallas_call(
         functools.partial(kernel, n_rep, n_blk, n_tp),
         out_shape=(
@@ -431,18 +473,19 @@
         out_specs=(vmem, vmem, anywhere),
         scratch_shapes=[
             pltpu.VMEM((LAYERS, 3, model, width), bf16),
-            pltpu.VMEM((LAYERS, model, n_ff * width), bf16),
+            pltpu.VMEM((LAYERS, model, ff), bf16),
             pltpu.VMEM((LAYERS, width, model), bf16),
-            pltpu.VMEM((LAYERS, 2, n_ff // 2 * width, model), bf16),
+            pltpu.VMEM((LAYERS, ff, model), bf16),
             pltpu.VMEM((LAYERS, 2, slots + extra, PAGE, width), bf16),
             pltpu.VMEM((LAYERS, n_blk, 4, 2 * rows, width), f32),
-            pltpu.VMEM((LAYERS, n_blk, n_ff, 2 * rows, width), f32),
+            pltpu.VMEM((LAYERS, n_blk, rows * n_rep + 8, ff + 128), f32),
             pltpu.VMEM((LAYERS, n_rep, 4 * rows, width // 4), bf16),
             pltpu.VMEM((LAYERS, n_rep, 4 * rows, width // 4 + 128), bf16),
             pltpu.VMEM((LAYERS, n_all, 4 * rows, width // 4 + 128), bf16),
             pltpu.VMEM((LAYERS, n_tp, 16, c_width), bf16),
-            pltpu.VMEM((2 * rows, model), f32),
-            pltpu.VMEM((n_ff, 2 * rows, width), bf16),
+            pltpu.VMEM((LAYERS, n_rep, 16, c_width), bf16),
+            pltpu.VMEM((LAYERS, n_rep, 2 * rows, m_width), f32),
+            pltpu.VMEM((LAYERS, n_rep, 2 * rows, m_width), f32),
             pltpu.VMEM((width // HD * rows * n_rep, (slots + extra) * PAGE), f32),
             pltpu.VMEM((slots, PAGE, width), bf16),
             dma((n_copies,)), dma((1,)),
@@ -451,6 +494,8 @@
             dma((LAYERS, n_rep)), dma((LAYERS, n_rep)),
             dma((LAYERS, n_all)), dma((LAYERS, n_all)),
             dma((LAYERS, n_tp)), dma((LAYERS, n_tp)),
+            dma((LAYERS, n_rep)), dma((LAYERS, n_rep)),
+            dma((LAYERS, n_rep)), dma((LAYERS, n_rep)),
         ],
         compiler_params=pltpu.CompilerParams(
             collective_id=0, has_side_effects=True, vmem_limit_bytes=56 * 2**20),

time: 36.7 us -> 37.7 us (1.027)
  Pallas kernels: 32.4 us -> 33.4 us
    pallas_call x1, Pallas kernels: 32.4 us -> 33.4 us  [per_device(): pl.pallas_call(functools.partial(kernel, n_rep, n_blk, n_tp), out_shape=(...]
where the time goes in v4:
time: 37.7 us; the launch traced here: 37.5 us
  Pallas kernels  33.4 us (89%)
  other arithmetic  3.38 us (9%)
  between operations  0.65 us (2%)
    pallas_call x1, Pallas kernels, per_device(): pl.pallas_call(functools.partial(kernel, n_rep, n_blk, n_tp), out_shape=(...  33.4 us
    select_n x1, other arithmetic, per_device(): jnp.where(caches < bound[None, None], caches, fresh[:, :, :, None, :])  2.06 us
    convert_element_type x1, other arithmetic, per_device(): return (state.astype(bf16), caches_out)  1.32 us

profile of v4, /device:TPU:0, one launch (start us, length us, event | category | flops | bytes accessed | tf_op | source)
XLA Modules:
  0.0 37.5 jit_solution(14614328644286981279)
XLA Ops:
  0.6 0.0 copy-start
  0.6 33.4 %decode_layers.1 = (f32[4,1024]{1,0:T(4,128)}, bf16[2,2,8,512]{3,2,1,0:T(8,128)(2,1)}, bf16[8,32,512]{2,1,0:T(8,128)(2,1)}) custom-call(s32[8]{0:T(128)} %owner_ref.1, s32[8]{0:T(128)} %used_ref.1, s32[8]{0:T(128)} %fill_ref.1, s32[8]{0:T(128)} %tail_ref.1, s32[4]{0:T(128)} %pos_ref.1, bf16[4,1024]{1,0:T(4,128)(2,1)} %hidden_ref.1, f32[2,1024]{1,0:T(2,128)} %gain_ref.1, ...), custom_call_target="tpu_custom_call" | custom-call | tf_op jit(solution)/shard_map/decode_layers/pallas_call | solution.py:465
  34.1 1.3 %convert_element_type.3 = bf16[4,1024]{1,0:T(4,128)(2,1)} convert(f32[4,1024]{1,0:T(4,128)} %get-tuple-element.5) | non-fusion elementwise | flops 4096 | bytes 24576 | tf_op jit(solution)/shard_map/convert_element_type | solution.py:509
  35.4 0.0 copy-done
  35.4 2.1 %compare_select_fusion = bf16[2,2,8,32,512]{4,3,2,1,0:T(8,128)(2,1)} fusion(bf16[2,2,8,32,512]{4,3,2,1,0:T(8,128)(2,1)S(1)} %copy-done, bf16[2,2,8,512]{3,2,1,0:T(8,128)(2,1)} %get-tuple-element.7, bf16[8,32,512]{2,1,0:T(8,128)(2,1)} %get-tuple-element.6), kind=kLoop, calls=%fused_computation | loop fusion | flops 1048576 | bytes 2392064 | tf_op jit(solution)/shard_map/jit(_where)/select_n | solution.py:508
Async XLA Ops:
  0.6 34.8 %copy-start = (bf16[2,2,8,32,512]{4,3,2,1,0:T(8,128)(2,1)S(1)}, bf16[2,2,8,32,512]{4,3,2,1,0:T(8,128)(2,1)}, u32[]{:S(2)}) copy-start(bf16[2,2,8,32,512]{4,3,2,1,0:T(8,128)(2,1)} %cache_hbm.1) | copy-start | bytes 3145732

commit v5 on v3

--- a/solution.py
+++ b/solution.py
@@ -47,10 +47,10 @@
     owner_ref, used_ref, fill_ref, tail_ref, pos_ref,
     hidden_ref, gain_ref, freq_ref,
     wqkv_hbm, wfc1_hbm, wout_hbm, wfc2_hbm, cache_hbm,
-    state_ref, fresh_ref, bound_hbm,
+    state_ref, fresh_ref,
     wqkv, wfc1, wout, wfc2, cache,
-    buf_a, buf_i, buf_q, msg, buf_b, buf_c, mlp_acc, act_ref, mask_ref, bound_ref,
-    w_sem, o_sem, a_send, a_recv, i_send, i_recv, q_send, q_recv, b_send, b_recv, c_send, c_recv,
+    buf_a, buf_i, buf_q, msg, buf_b, buf_c, mlp_acc, act_ref, mask_ref,
+    w_sem, a_send, a_recv, i_send, i_recv, q_send, q_recv, b_send, b_recv, c_send, c_recv,
 ):
     f32, bf16 = jnp.float32, jnp.bfloat16
     rows, model = hidden_ref.shape
@@ -165,11 +165,6 @@
         home = jnp.where(row_iota((slots, width)) == s, home_row, home)
         new_lane = jnp.where(tail_ref[s] == 1, slots * PAGE + home_row, -1)
         col_owner = jnp.where(lanes == new_lane, owner_ref[s], col_owner)
-        write_pos = jnp.where(tail_ref[s] == 1, fill_ref[s], -1)
-        bound_ref[s] = jnp.where(
-            row_iota((PAGE, width)) == write_pos, -jnp.inf, jnp.inf).astype(bf16)
-    bound_copy = pltpu.make_async_copy(bound_ref, bound_hbm, o_sem.at[0])
-    bound_copy.start()
     mask_ref[...] = jnp.where(
         lax.rem(row_iota((heads * reqs, columns)), reqs) == col_owner, 1.0, 0.0)
     for l in range(LAYERS):
@@ -377,6 +372,12 @@
                 fresh = jnp.where(home == r, new[i][r:r + 1], fresh)
             fresh_ref[l, i] = fresh.astype(bf16)
 
+        each(1, n_blk, lambda k: copy_a(l, 0)(k).wait_send())
+        each(1, n_blk, lambda k: copy_a(l, 1)(k).wait_send())
+        each(1, n_blk, lambda k: copy_i(l)(k).wait_send())
+        each(1, n_rep, lambda k: copy_q(l)(k).wait_send())
+        each(1, n_all, lambda k: copy_b(l)(k).wait_send())
+
         each(1, n_tp, lambda k: copy_c(l)(k).wait_recv())
         total = buf_c[l, lax.rem(my_tp + n_tp, n_tp)].astype(f32)
         for t in range(1, n_tp):
@@ -385,14 +386,19 @@
         state = (state + total).astype(bf16).astype(f32)
 
     state_ref[...] = state
-    bound_copy.wait()
     for l in range(LAYERS):
-        each(1, n_blk, lambda k: copy_a(l, 0)(k).wait_send())
-        each(1, n_blk, lambda k: copy_a(l, 1)(k).wait_send())
-        each(1, n_blk, lambda k: copy_i(l)(k).wait_send())
-        each(1, n_rep, lambda k: copy_q(l)(k).wait_send())
-        each(1, n_all, lambda k: copy_b(l)(k).wait_send())
         each(1, n_tp, lambda k: copy_c(l)(k).wait_send())
+
+
+def page_kernel(fill_ref, tail_ref, state_in, fresh_ref, cache_ref, state_ref, out_ref):
+    page_shape = cache_ref.shape[3:]
+    state_ref[...] = state_in[...].astype(state_ref.dtype)
+    for s in range(cache_ref.shape[2]):
+        write_pos = jnp.where(tail_ref[s] == 1, fill_ref[s], -1)
+        page = cache_ref[0, 0, s].astype(jnp.float32)
+        fresh = fresh_ref[0, 0, s:s + 1].astype(jnp.float32)
+        out_ref[0, 0, s] = jnp.where(
+            row_iota(page_shape) == write_pos, fresh, page).astype(out_ref.dtype)
 
 
 def frequencies(rows):
@@ -420,15 +426,14 @@
     anywhere = pl.BlockSpec(memory_space=pl.ANY)
     dma = pltpu.SemaphoreType.DMA
     n_copies = LAYERS * (3 + n_ff + 2 + 2 + 1)
-    state, fresh, bound = pl.pallas_call(
+    state, fresh = pl.pallas_call(
         functools.partial(kernel, n_rep, n_blk, n_tp),
         out_shape=(
             jax.ShapeDtypeStruct((rows, model), f32),
             jax.ShapeDtypeStruct((LAYERS, 2, slots, width), bf16),
-            jax.ShapeDtypeStruct((slots, PAGE, width), bf16),
         ),
         in_specs=[smem] * 5 + [vmem] * 3 + [anywhere] * 5,
-        out_specs=(vmem, vmem, anywhere),
+        out_specs=(vmem, vmem),
         scratch_shapes=[
             pltpu.VMEM((LAYERS, 3, model, width), bf16),
             pltpu.VMEM((LAYERS, model, n_ff * width), bf16),
@@ -444,8 +449,7 @@
             pltpu.VMEM((2 * rows, model), f32),
             pltpu.VMEM((n_ff, 2 * rows, width), bf16),
             pltpu.VMEM((width // HD * rows * n_rep, (slots + extra) * PAGE), f32),
-            pltpu.VMEM((slots, PAGE, width), bf16),
-            dma((n_copies,)), dma((1,)),
+            dma((n_copies,)),
             dma((LAYERS, n_blk, 2)), dma((LAYERS, n_blk, 2)),
             dma((LAYERS, n_blk)), dma((LAYERS, n_blk)),
             dma((LAYERS, n_rep)), dma((LAYERS, n_rep)),
@@ -460,8 +464,24 @@
         hidden, ln_gain, jnp.asarray(frequencies(2 * rows)),
         wq, w_fc1, w_out, w_fc2, caches,
     )
-    caches_out = jnp.where(caches < bound[None, None], caches, fresh[:, :, :, None, :])
-    return (state.astype(bf16), caches_out)
+    block = pl.BlockSpec(
+        (1, 1, slots, PAGE, width), lambda l, i: (l, i, 0, 0, 0))
+    return pl.pallas_call(
+        page_kernel,
+        grid=(LAYERS, 2),
+        out_shape=(
+            jax.ShapeDtypeStruct((rows, model), bf16),
+            jax.ShapeDtypeStruct(caches.shape, bf16),
+        ),
+        in_specs=[
+            smem, smem,
+            pl.BlockSpec((rows, model), lambda l, i: (0, 0)),
+            pl.BlockSpec((1, 1, slots, width), lambda l, i: (l, i, 0, 0)),
+            block,
+        ],
+        out_specs=(pl.BlockSpec((rows, model), lambda l, i: (0, 0)), block),
+        name="write_pages",
+    )(page_fill, page_tail, state, fresh, caches)
 
 
 def solution(mesh):

time: 36.7 us -> 36.7 us (level)
  Pallas kernels: 32.4 us -> 35.9 us
  other arithmetic: 3.38 us -> 0 us
    pallas_call x0 -> x1, Pallas kernels: none -> 3.52 us  [per_device(): pl.pallas_call(page_kernel, grid=(LAYERS, 2), out_shape=(jax.ShapeDtypeSt...]
    select_n x1 -> x0, other arithmetic: 2.06 us -> none  [per_device(): jnp.where(caches < bound[None, None], caches, fresh[:, :, :, None, :])]
    convert_element_type x1 -> x0, other arithmetic: 1.32 us -> none  [per_device(): return (state.astype(bf16), caches_out)]
where the time goes in v5:
time: 36.7 us; the launch traced here: 36.5 us
  Pallas kernels  35.9 us (98%)
  between operations  0.64 us (2%)
    pallas_call x1, Pallas kernels, per_device(): pl.pallas_call(functools.partial(kernel, n_rep, n_blk, n_tp), out_shape=(...  32.3 us
    pallas_call x1, Pallas kernels, per_device(): pl.pallas_call(page_kernel, grid=(LAYERS, 2), out_shape=(jax.ShapeDtypeSt...  3.52 us

profile of v5, /device:TPU:0, one launch (start us, length us, event | category | flops | bytes accessed | tf_op | source)
XLA Modules:
  0.0 36.5 jit_solution(7513230476480641061)
XLA Ops:
  0.6 32.3 %decode_layers.1 = (f32[4,1024]{1,0:T(4,128)}, bf16[2,2,8,512]{3,2,1,0:T(8,128)(2,1)}) custom-call(s32[8]{0:T(128)} %owner_ref.1, s32[8]{0:T(128)} %used_ref.1, s32[8]{0:T(128)} %fill_ref.3, s32[8]{0:T(128)} %tail_ref.3, s32[4]{0:T(128)} %pos_ref.1, bf16[4,1024]{1,0:T(4,128)(2,1)} %hidden_ref.1, f32[2,1024]{1,0:T(2,128)} %gain_ref.1, ...), custom_call_target="tpu_custom_call" | custom-call | tf_op jit(solution)/shard_map/decode_layers/pallas_call | solution.py:429
  33.0 3.5 %write_pages.1 = (bf16[4,1024]{1,0:T(4,128)(2,1)}, bf16[2,2,8,32,512]{4,3,2,1,0:T(8,128)(2,1)}) custom-call(s32[8]{0:T(128)} %fill_ref.3, s32[8]{0:T(128)} %tail_ref.3, f32[4,1024]{1,0:T(4,128)} %get-tuple-element.4.state_in, bf16[2,2,8,512]{3,2,1,0:T(8,128)(2,1)} %get-tuple-element.5.fresh_ref, bf16[2,2,8,32,512]{4,3,2,1,0:T(8,128)(2,1)} %cache_ref.1), custom_call_target="tpu_custom_call" | custom-call | tf_op jit(solution)/shard_map/write_pages/pallas_call | solution.py:469

commit v6 on v3

--- a/solution.py
+++ b/solution.py
@@ -47,10 +47,10 @@
     owner_ref, used_ref, fill_ref, tail_ref, pos_ref,
     hidden_ref, gain_ref, freq_ref,
     wqkv_hbm, wfc1_hbm, wout_hbm, wfc2_hbm, cache_hbm,
-    state_ref, fresh_ref, bound_hbm,
+    state_ref, fresh_ref, bound_ref,
     wqkv, wfc1, wout, wfc2, cache,
-    buf_a, buf_i, buf_q, msg, buf_b, buf_c, mlp_acc, act_ref, mask_ref, bound_ref,
-    w_sem, o_sem, a_send, a_recv, i_send, i_recv, q_send, q_recv, b_send, b_recv, c_send, c_recv,
+    buf_a, buf_i, buf_q, msg, buf_b, buf_c, mlp_acc, act_ref, mask_ref,
+    w_sem, a_send, a_recv, i_send, i_recv, q_send, q_recv, b_send, b_recv, c_send, c_recv,
 ):
     f32, bf16 = jnp.float32, jnp.bfloat16
     rows, model = hidden_ref.shape
@@ -168,8 +168,6 @@
         write_pos = jnp.where(tail_ref[s] == 1, fill_ref[s], -1)
         bound_ref[s] = jnp.where(
             row_iota((PAGE, width)) == write_pos, -jnp.inf, jnp.inf).astype(bf16)
-    bound_copy = pltpu.make_async_copy(bound_ref, bound_hbm, o_sem.at[0])
-    bound_copy.start()
     mask_ref[...] = jnp.where(
         lax.rem(row_iota((heads * reqs, columns)), reqs) == col_owner, 1.0, 0.0)
     for l in range(LAYERS):
@@ -377,6 +375,12 @@
                 fresh = jnp.where(home == r, new[i][r:r + 1], fresh)
             fresh_ref[l, i] = fresh.astype(bf16)
 
+        each(1, n_blk, lambda k: copy_a(l, 0)(k).wait_send())
+        each(1, n_blk, lambda k: copy_a(l, 1)(k).wait_send())
+        each(1, n_blk, lambda k: copy_i(l)(k).wait_send())
+        each(1, n_rep, lambda k: copy_q(l)(k).wait_send())
+        each(1, n_all, lambda k: copy_b(l)(k).wait_send())
+
         each(1, n_tp, lambda k: copy_c(l)(k).wait_recv())
         total = buf_c[l, lax.rem(my_tp + n_tp, n_tp)].astype(f32)
         for t in range(1, n_tp):
@@ -385,13 +389,7 @@
         state = (state + total).astype(bf16).astype(f32)
 
     state_ref[...] = state
-    bound_copy.wait()
     for l in range(LAYERS):
-        each(1, n_blk, lambda k: copy_a(l, 0)(k).wait_send())
-        each(1, n_blk, lambda k: copy_a(l, 1)(k).wait_send())
-        each(1, n_blk, lambda k: copy_i(l)(k).wait_send())
-        each(1, n_rep, lambda k: copy_q(l)(k).wait_send())
-        each(1, n_all, lambda k: copy_b(l)(k).wait_send())
         each(1, n_tp, lambda k: copy_c(l)(k).wait_send())
 
 
@@ -423,12 +421,12 @@
     state, fresh, bound = pl.pallas_call(
         functools.partial(kernel, n_rep, n_blk, n_tp),
         out_shape=(
-            jax.ShapeDtypeStruct((rows, model), f32),
-            jax.ShapeDtypeStruct((LAYERS, 2, slots, width), bf16),
-            jax.ShapeDtypeStruct((slots, PAGE, width), bf16),
+            pltpu.VMEM((rows, model), f32),
+            pltpu.VMEM((LAYERS, 2, slots, width), bf16),
+            pltpu.VMEM((slots, PAGE, width), bf16),
         ),
         in_specs=[smem] * 5 + [vmem] * 3 + [anywhere] * 5,
-        out_specs=(vmem, vmem, anywhere),
+        out_specs=(vmem, vmem, vmem),
         scratch_shapes=[
             pltpu.VMEM((LAYERS, 3, model, width), bf16),
             pltpu.VMEM((LAYERS, model, n_ff * width), bf16),
@@ -444,8 +442,7 @@
             pltpu.VMEM((2 * rows, model), f32),
             pltpu.VMEM((n_ff, 2 * rows, width), bf16),
             pltpu.VMEM((width // HD * rows * n_rep, (slots + extra) * PAGE), f32),
-            pltpu.VMEM((slots, PAGE, width), bf16),
-            dma((n_copies,)), dma((1,)),
+            dma((n_copies,)),
             dma((LAYERS, n_blk, 2)), dma((LAYERS, n_blk, 2)),
             dma((LAYERS, n_blk)), dma((LAYERS, n_blk)),
             dma((LAYERS, n_rep)), dma((LAYERS, n_rep)),
@@ -453,7 +450,7 @@
             dma((LAYERS, n_tp)), dma((LAYERS, n_tp)),
         ],
         compiler_params=pltpu.CompilerParams(
-            collective_id=0, has_side_effects=True, vmem_limit_bytes=56 * 2**20),
+            collective_id=0, has_side_effects=True, vmem_limit_bytes=57 * 2**20),
         name="decode_layers",
     )(
         page_owner, page_used, page_fill, page_tail, positions,

time: 36.7 us -> 34.2 us (0.932)
  other arithmetic: 3.38 us -> 1.69 us
  Pallas kernels: 32.4 us -> 31.7 us
    select_n x1, other arithmetic: 2.06 us -> 1.09 us  [per_device(): jnp.where(caches < bound[None, None], caches, fresh[:, :, :, None, :])]
    convert_element_type x1, other arithmetic: 1.32 us -> 0.6 us  [per_device(): return (state.astype(bf16), caches_out)]
    pallas_call x1, Pallas kernels: 32.4 us -> 31.7 us  [per_device(): pl.pallas_call(functools.partial(kernel, n_rep, n_blk, n_tp), out_shape=(...]
where the time goes in v6:
time: 34.2 us; the launch traced here: 34.1 us
  Pallas kernels  31.7 us (93%)
  other arithmetic  1.69 us (5%)
  between operations  0.65 us (2%)
    pallas_call x1, Pallas kernels, per_device(): pl.pallas_call(functools.partial(kernel, n_rep, n_blk, n_tp), out_shape=(...  31.7 us
    select_n x1, other arithmetic, per_device(): jnp.where(caches < bound[None, None], caches, fresh[:, :, :, None, :])  1.09 us

profile of v6, /device:TPU:0, one launch (start us, length us, event | category | flops | bytes accessed | tf_op | source)
XLA Modules:
  0.0 34.1 jit_solution(11707492104351865491)
XLA Ops:
  0.6 0.0 copy-start
  0.6 31.7 %decode_layers.1 = (f32[4,1024]{1,0:T(4,128)S(1)}, bf16[2,2,8,512]{3,2,1,0:T(8,128)(2,1)S(1)}, bf16[8,32,512]{2,1,0:T(8,128)(2,1)S(1)}) custom-call(s32[8]{0:T(128)} %owner_ref.1, s32[8]{0:T(128)} %used_ref.1, s32[8]{0:T(128)} %fill_ref.1, s32[8]{0:T(128)} %tail_ref.1, s32[4]{0:T(128)} %pos_ref.1, bf16[4,1024]{1,0:T(4,128)(2,1)} %hidden_ref.1, ...), custom_call_target="tpu_custom_call" | custom-call | tf_op jit(solution)/shard_map/decode_layers/pallas_call | solution.py:421
  32.4 0.6 %convert_element_type.3 = bf16[4,1024]{1,0:T(4,128)(2,1)} convert(f32[4,1024]{1,0:T(4,128)S(1)} %get-tuple-element.5) | non-fusion elementwise | flops 4096 | bytes 24576 | tf_op jit(solution)/shard_map/convert_element_type | solution.py:461
  33.0 0.0 copy-done
  33.0 1.1 %compare_select_fusion = bf16[2,2,8,32,512]{4,3,2,1,0:T(8,128)(2,1)} fusion(bf16[2,2,8,32,512]{4,3,2,1,0:T(8,128)(2,1)S(1)} %copy-done, bf16[2,2,8,512]{3,2,1,0:T(8,128)(2,1)S(1)} %get-tuple-element.7, bf16[8,32,512]{2,1,0:T(8,128)(2,1)S(1)} %get-tuple-element.6), kind=kLoop, calls=%fused_computation | loop fusion | flops 1048576 | bytes 2392064 | tf_op jit(solution)/shard_map/jit(_where)/select_n | solution.py:460
Async XLA Ops:
  0.6 32.4 %copy-start = (bf16[2,2,8,32,512]{4,3,2,1,0:T(8,128)(2,1)S(1)}, bf16[2,2,8,32,512]{4,3,2,1,0:T(8,128)(2,1)}, u32[]{:S(2)}) copy-start(bf16[2,2,8,32,512]{4,3,2,1,0:T(8,128)(2,1)} %cache_hbm.1) | copy-start | bytes 3145732

commit v7 on v6

--- a/solution.py
+++ b/solution.py
@@ -280,8 +280,6 @@
         for c in range(ff_half, n_ff):
             project_ff(c)
         each(1, n_blk, lambda k: copy_i(l)(k).start())
-        if l + 1 < LAYERS:
-            got[l + 1] = bring_layer(l + 1, 1)
         each(1, n_blk, lambda k: copy_a(l, 1)(k).wait_recv())
         new_k = rotate(jnp.concatenate([finish(buf_a, 2), blank], axis=0))[:rows]
         new_v = finish(buf_a, 3).astype(bf16).astype(f32)
@@ -334,6 +332,8 @@
                 [fold(out[part]), jnp.concatenate([stat[part] for stat in stats], axis=0)],
                 axis=1).astype(bf16)
         each(1, n_all, lambda k: copy_b(l)(k).start())
+        if l + 1 < LAYERS:
+            got[l + 1] = bring_layer(l + 1, 1)
         buf_b[l, 0] = msg[l, my_rep]
 
         g["fc2"][1].wait()

time: 34.2 us -> 34.2 us (level)
  no operation moved by 1% of the time
where the time goes in v7:
time: 34.2 us; the launch traced here: 34.1 us
  Pallas kernels  31.7 us (93%)
  other arithmetic  1.69 us (5%)
  between operations  0.65 us (2%)
    pallas_call x1, Pallas kernels, per_device(): pl.pallas_call(functools.partial(kernel, n_rep, n_blk, n_tp), out_shape=(...  31.7 us
    select_n x1, other arithmetic, per_device(): jnp.where(caches < bound[None, None], caches, fresh[:, :, :, None, :])  1.09 us

profile of v7, /device:TPU:0, one launch (start us, length us, event | category | flops | bytes accessed | tf_op | source)
XLA Modules:
  0.0 34.1 jit_solution(11842537570954957010)
XLA Ops:
  0.6 0.0 copy-start
  0.6 31.7 %decode_layers.1 = (f32[4,1024]{1,0:T(4,128)S(1)}, bf16[2,2,8,512]{3,2,1,0:T(8,128)(2,1)S(1)}, bf16[8,32,512]{2,1,0:T(8,128)(2,1)S(1)}) custom-call(s32[8]{0:T(128)} %owner_ref.1, s32[8]{0:T(128)} %used_ref.1, s32[8]{0:T(128)} %fill_ref.1, s32[8]{0:T(128)} %tail_ref.1, s32[4]{0:T(128)} %pos_ref.1, bf16[4,1024]{1,0:T(4,128)(2,1)} %hidden_ref.1, ...), custom_call_target="tpu_custom_call" | custom-call | tf_op jit(solution)/shard_map/decode_layers/pallas_call | solution.py:421
  32.4 0.6 %convert_element_type.3 = bf16[4,1024]{1,0:T(4,128)(2,1)} convert(f32[4,1024]{1,0:T(4,128)S(1)} %get-tuple-element.5) | non-fusion elementwise | flops 4096 | bytes 24576 | tf_op jit(solution)/shard_map/convert_element_type | solution.py:461
  33.0 0.0 copy-done
  33.0 1.1 %compare_select_fusion = bf16[2,2,8,32,512]{4,3,2,1,0:T(8,128)(2,1)} fusion(bf16[2,2,8,32,512]{4,3,2,1,0:T(8,128)(2,1)S(1)} %copy-done, bf16[2,2,8,512]{3,2,1,0:T(8,128)(2,1)S(1)} %get-tuple-element.7, bf16[8,32,512]{2,1,0:T(8,128)(2,1)S(1)} %get-tuple-element.6), kind=kLoop, calls=%fused_computation | loop fusion | flops 1048576 | bytes 2392064 | tf_op jit(solution)/shard_map/jit(_where)/select_n | solution.py:460
Async XLA Ops:
  0.6 32.4 %copy-start = (bf16[2,2,8,32,512]{4,3,2,1,0:T(8,128)(2,1)S(1)}, bf16[2,2,8,32,512]{4,3,2,1,0:T(8,128)(2,1)}, u32[]{:S(2)}) copy-start(bf16[2,2,8,32,512]{4,3,2,1,0:T(8,128)(2,1)} %cache_hbm.1) | copy-start | bytes 3145732
